TPU v7x, 512 devices: a whole 4x4x16 slice. The times are simulated.
512 devices in a mesh: tower: 2 (over core), tp: 16 (over z), grp: 16 (over y, x).
Axes of the slice: x: 4, y: 4, z: 16, core: 2. Of those that a mesh axis runs over, the one named last changes fastest.
Arguments:
- tokens: bfloat16 [12288, 8192], P('grp', 'tp'), may hold values from -700 to 700
- modality: int32 [12288], P('grp'), may hold values from 0 to 1, as said below
- doc_ids: int32 [12288], P('grp'), may hold values from 0 to 255, as said below
- owner_ids: int32 [12288], P('grp'), may hold values from 0 to 15, as said below
- norm_gain: float32 [2, 8192], P('tower'), may hold values from 0.5 to 1.5
- query_weight: bfloat16 [2, 8192, 4096], P('tower', 'grp', 'tp'), may hold values from -0.125 to 0.125
- pair_weight: bfloat16 [2, 8192, 1024], P('tower', 'grp'), may hold values from -0.125 to 0.125
Outputs:
- attended: bfloat16 [2, 12288, 4096], P('tower', 'grp', 'tp')
Inputs may be any that keep to these rules, and one draw needn't show every extreme that they name: Every group of 768 tokens holds exactly 384 tokens of each modality. `owner_ids`: within every group each owner is named by exactly 48 tokens, and by at most 48 tokens of one modality. `doc_ids`: all tokens of one document have the same owner.
All inputs are finite; a program needn't handle non-finite values.
Results may differ from a plain program's by a relative error of at most 0.0084.
Values may be sent and summed in bfloat16 or wider, within the bound.
No kernel may reach another device: no remote copies, remote signals or barrier semaphores. Data moves between devices by JAX's collectives and lax.ppermute only.
A program may use at most 64 MiB of HBM per device.

v0:
```python
import math

import jax
import jax.numpy as jnp
from jax import lax
from jax.sharding import PartitionSpec as P

HD = 128


EPS = 1e-05
MASKED = -1e30


def in_one_piece(arrays, axis, dim, along):
    both = jnp.concatenate(arrays, axis=along)
    whole, at, finished = (lax.all_gather(both, axis, axis=dim, tiled=True), 0, [])
    for a in arrays:
        finished.append(lax.slice_in_dim(whole, at, at + a.shape[along], axis=along))
        at += a.shape[along]
    return tuple(finished)


def sent_together(arrays, axis, split_dim, concat_dim, along):
    widths = [a.shape[along] for a in arrays]
    both = jnp.concatenate(arrays, axis=along)
    whole = lax.all_to_all(both, axis, split_axis=split_dim, concat_axis=concat_dim, tiled=True)
    return tuple(jnp.split(whole, [sum(widths[:k]) for k in range(1, len(widths))], axis=along))


def from_partner(value, axis, stride):
    mask = 2**stride
    pairs = [(source, source ^ mask) for source in range(lax.axis_size(axis))]
    return lax.ppermute(value, axis, pairs)


def local(tokens, modality, doc_ids, owner_ids, norm_gain, query_weight, pair_weight):
    groups = lax.axis_size("grp")
    tp_count = lax.axis_size("tp")
    tower_index = lax.axis_index("tower")
    group_index = lax.axis_index("grp")
    tp_rank = lax.axis_index("tp")
    tok_count = tokens.shape[0]
    half_rows = tok_count // 2
    slot_count = tok_count // groups
    total_slots = groups * slot_count
    head_cols = query_weight.shape[2]
    pair_cols = pair_weight.shape[2]
    pair_heads = pair_cols // (2 * HD)
    own_head = tp_rank // (tp_count // pair_heads)
    in_tower = modality == tower_index
    positions = jnp.arange(tok_count, dtype=jnp.int32)
    packed_rank = jnp.cumsum(in_tower.astype(jnp.int32)) - 1
    row_index = (
        jnp.zeros((half_rows,), jnp.int32)
        .at[jnp.where(in_tower, packed_rank, half_rows)]
        .set(positions, mode="drop")
    )
    chosen = tokens[row_index]
    features = lax.all_gather(chosen, "tp", axis=1, tiled=True)
    values = features.astype(jnp.float32)
    inverse_rms = lax.rsqrt(jnp.mean(values * values, axis=1, keepdims=True) + EPS)
    normed = (values * inverse_rms * norm_gain[0][None, :]).astype(jnp.bfloat16)
    query_local = query_weight[0]
    pair_local = pair_weight[0]
    pair_part = lax.dynamic_slice_in_dim(pair_local, own_head * 2 * HD, 2 * HD, 1)
    pieces = in_one_piece((query_local, pair_part), "grp", 0, 1)
    totals = tuple(
        (jnp.dot(normed, weight_rows, preferred_element_type=jnp.float32) for weight_rows in pieces)
    )
    query_rows = totals[0].astype(jnp.bfloat16)
    pair_rows = totals[1].astype(jnp.bfloat16)
    owner_onehot = (
        (owner_ids[:, None] == jnp.arange(groups, dtype=jnp.int32)[None, :]) & in_tower[:, None]
    ).astype(jnp.int32)
    slot_rank = jnp.sum((jnp.cumsum(owner_onehot, axis=0) - 1) * owner_onehot, axis=1)
    destination = jnp.where(in_tower, owner_ids * slot_count + slot_rank, total_slots)
    source_row = (
        jnp.full((total_slots,), half_rows, jnp.int32).at[destination].set(packed_rank, mode="drop")
    )
    filled = source_row < half_rows
    safe_row = jnp.minimum(source_row, half_rows - 1)
    zero_value = jnp.zeros((), jnp.bfloat16)
    query_send = jnp.where(filled[:, None], query_rows[safe_row], zero_value)
    pair_send = jnp.where(filled[:, None], pair_rows[safe_row], zero_value)
    token_row = row_index[safe_row]
    doc_send = jnp.where(filled, doc_ids[token_row], -1)
    place_send = jnp.where(filled, group_index * tok_count + token_row, -1)
    query_in, pair_in, doc_in, place_in = (
        *sent_together((query_send, pair_send), "grp", 0, 0, 1),
        lax.all_to_all(doc_send, "grp", split_axis=0, concat_axis=0, tiled=True),
        lax.all_to_all(place_send, "grp", split_axis=0, concat_axis=0, tiled=True),
    )
    pair_other, doc_other, place_other = from_partner((pair_in, doc_in, place_in), "tower", 0)
    key_rows = jnp.concatenate([pair_in[:, :HD], pair_other[:, :HD]], axis=0)
    value_rows = jnp.concatenate([pair_in[:, HD:], pair_other[:, HD:]], axis=0)
    doc_keys = jnp.concatenate([doc_in, doc_other], axis=0)
    place_keys = jnp.concatenate([place_in, place_other], axis=0)
    is_image = tower_index == 1
    image_keys = jnp.concatenate(
        [jnp.full((total_slots,), is_image), jnp.full((total_slots,), jnp.logical_not(is_image))],
        axis=0,
    )
    heads_here = head_cols // HD
    queries = query_in.reshape(total_slots, heads_here, HD)
    scores = jnp.einsum("qhd,kd->hqk", queries, key_rows, preferred_element_type=jnp.float32) * (
        1.0 / math.sqrt(HD)
    )
    allowed = (doc_in[:, None] == doc_keys[None, :]) & (
        (place_keys[None, :] <= place_in[:, None]) | is_image & image_keys[None, :]
    )
    scores = jnp.where(allowed[None], scores, MASKED)
    row_max = jnp.max(scores, axis=2, keepdims=True)
    powered = jnp.exp(scores - row_max)
    weights = (powered / jnp.sum(powered, axis=2, keepdims=True)).astype(jnp.bfloat16)
    mixed_rows = jnp.einsum("hqk,kd->qhd", weights, value_rows, preferred_element_type=jnp.float32)
    mixed_rows = mixed_rows.astype(jnp.bfloat16).reshape(total_slots, head_cols)
    returned = lax.all_to_all(mixed_rows, "grp", split_axis=0, concat_axis=0, tiled=True)
    safe_dest = jnp.minimum(destination, total_slots - 1)
    result = jnp.where(in_tower[:, None], returned[safe_dest], zero_value)
    return result[None]


def solution(mesh):
    in_specs = (
        P("grp", "tp"),
        P("grp"),
        P("grp"),
        P("grp"),
        P("tower", None),
        P("tower", "grp", "tp"),
        P("tower", "grp", None),
    )
    out_specs = P("tower", "grp", "tp")
    return jax.shard_map(local, mesh=mesh, in_specs=in_specs, out_specs=out_specs, check_vma=False)
```

profile of v0, /device:TPU:1, one launch (start us, length us, event | category | flops | bytes accessed | tf_op | source)
XLA Modules:
  0.0 289.1 jit_solution(18410098806642783935)
XLA Ops:
  12.1 3.4 %scatter_custom_fusion.1 = s32[384]{0:T(512)S(1)} fusion(s32[768]{0:T(1024)S(1)} %get-tuple-element.21, s32[768]{0:T(1024)S(1)} %iota.11, s32[]{:T(128)} %constant.27.clone.1), kind=kCustom, calls=%fused_computation.77 | custom fusion | bytes 1540 | tf_op jit(solution)/shard_map/scatter | solution.py:57
  15.5 3.8 %gather_fusion = bf16[384,512]{1,0:T(8,128)(2,1)} fusion(bf16[768,512]{1,0:T(8,128)(2,1)} %param.7, s32[1024]{0:T(1024)S(1)} %pad_clamp_fusion.3), kind=kCustom, calls=%fused_computation | custom fusion | bytes 787968 | tf_op jit(solution)/shard_map/gather | solution.py:59
  21.3 3.4 %scatter_custom_fusion = s32[768]{0:T(1024)S(1)} fusion(s32[768]{0:T(1024)S(1)} %get-tuple-element.18, s32[768]{0:T(1024)S(1)} %get-tuple-element.22, s32[]{:T(128)} %constant.25.clone.1), kind=kCustom, calls=%fused_computation.74 | custom fusion | bytes 3076 | tf_op jit(solution)/shard_map/scatter | solution.py:79
  24.7 5.0 %gather_fusion.3 = s32[768]{0:T(1024)S(1)} fusion(s32[384]{0:T(512)S(1)} %scatter_custom_fusion.1, s32[1024]{0:T(1024)S(1)} %pad_clamp_fusion.2), kind=kCustom, calls=%fused_computation.3 | custom fusion | bytes 9216 | tf_op jit(solution)/shard_map/gather | solution.py:86
  29.8 3.2 %gather_fusion.4 = s32[768]{0:T(1024)S(1)} fusion(s32[768]{0:T(1024)S(1)} %copy-done.1, s32[1024]{0:T(1024)S(1)} %pad_clamp_fusion.1), kind=kCustom, calls=%fused_computation.4 | custom fusion | bytes 9216 | tf_op jit(solution)/shard_map/gather | solution.py:87
  33.7 7.6 %all-to-all-start.2 = ((s32[16,48,1]{1,2,0:T(1,128)}), s32[16,48,1]{1,2,0:T(1,128)S(1)}, u32[]{:S(2)}, u32[]{:S(2)}) async-start(s32[16,48,1]{1,2,0:T(1,128)} %bitcast.12), calls=%async_computation.2 | async-start | bytes 16384 | tf_op jit(solution)/shard_map/all_to_all | solution.py:92
  42.0 66.6 %all-gather.6.cloned.1.call-done = bf16[384,8192]{1,0:T(8,128)(2,1)} async-done(((bf16[384,512]{1,0:T(8,128)(2,1)}), bf16[384,8192]{1,0:T(8,128)(2,1)}) %all-gather.6.cloned.1.call-update) | async-done | bytes 6291472 | tf_op jit(solution)/shard_map/all_gather | solution.py:60
  108.7 4.1 %fusion.1 = f32[384]{0:T(512)S(1)} fusion(bf16[384,8192]{1,0:T(8,128)(2,1)} %all-gather.6.cloned.1.call-done), kind=kLoop, calls=%fused_computation.11 | loop fusion | flops 9436800 | bytes 6292992 | tf_op jit(solution)/shard_map/reduce_sum | solution.py:62
  112.8 84.0 %all-gather.4.cloned.1.call-done = bf16[8192,512]{1,0:T(8,128)(2,1)} async-done(((bf16[512,512]{1,0:T(8,128)(2,1)}), bf16[8192,512]{1,0:T(8,128)(2,1)}) %all-gather.4.cloned.1.call-update) | async-done | bytes 8388624 | tf_op jit(solution)/shard_map/all_gather | solution.py:17
  196.7 5.9 %fusion.17 = bf16[384,256]{1,0:T(8,128)(2,1)S(1)} fusion(bf16[8192,512]{1,0:T(8,128)(2,1)} %all-gather.4.cloned.1.call-done, bf16[384,8192]{1,0:T(8,128)(2,1)} %all-gather.6.cloned.1.call-done, f32[8192]{0:T(1024)S(1)} %bitcast.79, f32[384]{0:T(512)S(1)} %add_rsqrt_fusion), kind=kOutput, calls=%fused_computation.29 | convolution fusion | flops 1623293952 | bytes 10716672 | tf_op jit(solution)/shard_map/dot_general | solution.py:69
  202.6 2.7 gather_fusion.1
  205.3 5.9 %fusion.22 = bf16[384,256]{1,0:T(8,128)(2,1)S(1)} fusion(bf16[8192,512]{1,0:T(8,128)(2,1)} %all-gather.4.cloned.1.call-done, bf16[384,8192]{1,0:T(8,128)(2,1)} %all-gather.6.cloned.1.call-done, f32[8192]{0:T(1024)S(1)} %bitcast.80, f32[384]{0:T(512)S(1)} %add_rsqrt_fusion), kind=kOutput, calls=%fused_computation.30 | convolution fusion | flops 1623293952 | bytes 10716672 | tf_op jit(solution)/shard_map/dot_general | solution.py:69
  211.1 2.7 gather_fusion.2
  214.0 5.0 %all-to-all-start.1 = ((s32[16,48,1]{1,2,0:T(1,128)}), s32[16,48,1]{1,2,0:T(1,128)S(1)}, u32[]{:S(2)}, u32[]{:S(2)}) async-start(s32[16,48,1]{1,2,0:T(1,128)} %bitcast.11), calls=%async_computation.1 | async-start | bytes 16384 | tf_op jit(solution)/shard_map/all_to_all | solution.py:91
  219.9 5.4 %all-to-all-done.1 = s32[16,48,1]{1,2,0:T(1,128)S(1)} async-done(((s32[16,48,1]{1,2,0:T(1,128)}), s32[16,48,1]{1,2,0:T(1,128)S(1)}, u32[]{:S(2)}, u32[]{:S(2)}) %all-to-all-start.1) | async-done | bytes 3104 | tf_op jit(solution)/shard_map/all_to_all | solution.py:91
  225.4 3.8 %all-to-all-start = ((bf16[16,48,512]{2,1,0:T(8,128)(2,1)}), bf16[16,48,512]{2,1,0:T(8,128)(2,1)S(1)}, u32[]{:S(2)}, u32[]{:S(2)}) async-start(bf16[16,48,512]{2,1,0:T(8,128)(2,1)} %pad_maximum_fusion), calls=%async_computation | async-start | bytes 1572864 | tf_op jit(solution)/shard_map/all_to_all | solution.py:27
  230.4 3.9 %collective-permute-start.1 = (s32[768]{0:T(1024)S(1)}, s32[768]{0:T(1024)S(1)}, u32[]{:S(2)}, u32[]{:S(2)}) collective-permute-start(s32[768]{0:T(1024)S(1)} %eq.60), channel_id=1, source_target_pairs={{0,256},{256,0},{1,257},{257,1},{2,258},{258,2},{3,259},{259,3},{4... | collective-permute-start | bytes 9224 | tf_op jit(solution)/shard_map/ppermute | solution.py:34
  238.1 3.5 %all-to-all-done = bf16[16,48,512]{2,1,0:T(8,128)(2,1)S(1)} async-done(((bf16[16,48,512]{2,1,0:T(8,128)(2,1)}), bf16[16,48,512]{2,1,0:T(8,128)(2,1)S(1)}, u32[]{:S(2)}, u32[]{:S(2)}) %all-to-all-start) | async-done | bytes 786464 | tf_op jit(solution)/shard_map/all_to_all | solution.py:27
  242.4 4.8 %collective-permute-start = (bf16[768,256]{1,0:T(8,128)(2,1)}, bf16[768,256]{1,0:T(8,128)(2,1)}, u32[]{:S(2)}, u32[]{:S(2)}) collective-permute-start(bf16[768,256]{1,0:T(8,128)(2,1)} %get-tuple-element.13), channel_id=1, source_target_pairs={{0,256},{256,0},{1,257},{257,1},{2,258},{258,2},{3,259},{259,3},{4... | collective-permute-start | bytes 1179656 | tf_op jit(solution)/shard_map/ppermute | solution.py:34
  250.9 8.3 %fusion.52 = (f32[2,768]{1,0:T(2,128)S(1)}, f32[2,768,1536]{1,2,0:T(8,128)}) fusion(pred[768,1536]{0,1:T(8,128)(4,1)S(1)} %or_and_fusion, bf16[768,2,128]{0,2,1:T(8,128)(2,1)} %bitcast.74, bf16[768,128]{1,0:T(8,128)(2,1)S(1)} %get-tuple-element.16, bf16[768,128]{1,0:T(8,128)(2,1)S(1)} %get-tuple-element.12), kind=kOutput, calls=%fused_computation.88 | convolution fusion | flops 614204928 | bytes 11409408 | tf_op jit(solution)/shard_map/sub | solution.py:114
  259.2 4.5 %fusion.16 = bf16[768,2,128]{0,2,1:T(8,128)(2,1)S(1)} fusion(f32[2,768,1536]{1,2,0:T(8,128)} %get-tuple-element.24, f32[2,768]{1,0:T(2,128)S(1)} %get-tuple-element.23, bf16[768,128]{1,0:T(8,128)(2,1)S(1)} %get-tuple-element.15, bf16[768,128]{1,0:T(8,128)(2,1)S(1)} %get-tuple-element.11), kind=kOutput, calls=%fused_computation.28 | convolution fusion | flops 609681408 | bytes 10229760 | tf_op jit(solution)/shard_map/hqk,kd->qhd/dot_general | solution.py:116
  265.1 3.6 %all-to-all-start.3 = ((bf16[16,48,256]{2,1,0:T(8,128)(2,1)}), bf16[16,48,256]{2,1,0:T(8,128)(2,1)S(1)}, u32[]{:S(2)}, u32[]{:S(2)}) async-start(bf16[16,48,256]{2,1,0:T(8,128)(2,1)} %all_to_all.35), calls=%async_computation.3 | async-start | bytes 786432 | tf_op jit(solution)/shard_map/all_to_all | solution.py:118
  268.7 9.9 %all-to-all-done.3 = bf16[16,48,256]{2,1,0:T(8,128)(2,1)S(1)} async-done(((bf16[16,48,256]{2,1,0:T(8,128)(2,1)}), bf16[16,48,256]{2,1,0:T(8,128)(2,1)S(1)}, u32[]{:S(2)}, u32[]{:S(2)}) %all-to-all-start.3) | async-done | bytes 393248 | tf_op jit(solution)/shard_map/all_to_all | solution.py:118
  278.7 2.6 gather_fusion.5
  (61 shorter events, 22.0 us)
Async XLA Ops:
  6.5 12.9 %copy-start = (bf16[1,512,1024]{2,1,0:T(8,128)(2,1)S(1)}, bf16[1,512,1024]{2,1,0:T(8,128)(2,1)}, u32[]{:S(2)}) copy-start(bf16[1,512,1024]{2,1,0:T(8,128)(2,1)} %param.13) | copy-start | bytes 3145732
  6.5 23.2 %copy-start.1 = (s32[768]{0:T(1024)S(1)}, s32[768]{0:T(1024)}, u32[]{:S(2)}) copy-start(s32[768]{0:T(1024)} %param.9) | copy-start | bytes 9220
  6.5 102.1 %all-gather.6.cloned.1.call-start = ((), (), s32[]{:S(2)}) async-start(), calls=%async_computation.5 | async-start | bytes 6684672 | tf_op jit(solution)/shard_map/all_gather | solution.py:60
  19.3 177.4 %all-gather.4.cloned.1.call-start = ((), (), s32[]{:S(2)}) async-start(), calls=%async_computation.4 | async-start | bytes 8912896 | tf_op jit(solution)/shard_map/all_gather | solution.py:17
  29.7 167.0 %copy-start.2 = (f32[1,8192]{1,0:T(1,128)S(1)}, f32[1,8192]{1,0:T(1,128)}, u32[]{:S(2)}) copy-start(f32[1,8192]{1,0:T(1,128)} %param.11) | copy-start | bytes 98308
  33.7 180.3 %all-to-all-start.2 = ((s32[16,48,1]{1,2,0:T(1,128)}), s32[16,48,1]{1,2,0:T(1,128)S(1)}, u32[]{:S(2)}, u32[]{:S(2)}) async-start(s32[16,48,1]{1,2,0:T(1,128)} %bitcast.12), calls=%async_computation.2 | async-start | bytes 16384 | tf_op jit(solution)/shard_map/all_to_all | solution.py:92
  214.0 11.4 %all-to-all-start.1 = ((s32[16,48,1]{1,2,0:T(1,128)}), s32[16,48,1]{1,2,0:T(1,128)S(1)}, u32[]{:S(2)}, u32[]{:S(2)}) async-start(s32[16,48,1]{1,2,0:T(1,128)} %bitcast.11), calls=%async_computation.1 | async-start | bytes 16384 | tf_op jit(solution)/shard_map/all_to_all | solution.py:91
  225.4 16.2 %all-to-all-start = ((bf16[16,48,512]{2,1,0:T(8,128)(2,1)}), bf16[16,48,512]{2,1,0:T(8,128)(2,1)S(1)}, u32[]{:S(2)}, u32[]{:S(2)}) async-start(bf16[16,48,512]{2,1,0:T(8,128)(2,1)} %pad_maximum_fusion), calls=%async_computation | async-start | bytes 1572864 | tf_op jit(solution)/shard_map/all_to_all | solution.py:27
  230.4 6.6 %collective-permute-start.1 = (s32[768]{0:T(1024)S(1)}, s32[768]{0:T(1024)S(1)}, u32[]{:S(2)}, u32[]{:S(2)}) collective-permute-start(s32[768]{0:T(1024)S(1)} %eq.60), channel_id=1, source_target_pairs={{0,256},{256,0},{1,257},{257,1},{2,258},{258,2},{3,259},{259,3},{4... | collective-permute-start | bytes 9224 | tf_op jit(solution)/shard_map/ppermute | solution.py:34
  235.1 3.1 %collective-permute-start.2 = (s32[768]{0:T(1024)S(1)}, s32[768]{0:T(1024)S(1)}, u32[]{:S(2)}, u32[]{:S(2)}) collective-permute-start(s32[768]{0:T(1024)S(1)} %all_to_all.34), channel_id=1, source_target_pairs={{0,256},{256,0},{1,257},{257,1},{2,258},{258,2},{3,259},{259,3},{4... | collective-permute-start | bytes 9224 | tf_op jit(solution)/shard_map/ppermute | solution.py:34
  242.4 7.5 %collective-permute-start = (bf16[768,256]{1,0:T(8,128)(2,1)}, bf16[768,256]{1,0:T(8,128)(2,1)}, u32[]{:S(2)}, u32[]{:S(2)}) collective-permute-start(bf16[768,256]{1,0:T(8,128)(2,1)} %get-tuple-element.13), channel_id=1, source_target_pairs={{0,256},{256,0},{1,257},{257,1},{2,258},{258,2},{3,259},{259,3},{4... | collective-permute-start | bytes 1179656 | tf_op jit(solution)/shard_map/ppermute | solution.py:34
  265.1 13.5 %all-to-all-start.3 = ((bf16[16,48,256]{2,1,0:T(8,128)(2,1)}), bf16[16,48,256]{2,1,0:T(8,128)(2,1)S(1)}, u32[]{:S(2)}, u32[]{:S(2)}) async-start(bf16[16,48,256]{2,1,0:T(8,128)(2,1)} %all_to_all.35), calls=%async_computation.3 | async-start | bytes 786432 | tf_op jit(solution)/shard_map/all_to_all | solution.py:118
Sparse Core Ops, SparseCore 0:
  19.5 89.1 all-gather.5
  111.7 85.0 all-gather.3
where the time goes:
time: 290 us; the launch traced here: 289 us
  waiting for transfers between devices  171 us (59%)
  local copies, waits for them, and re-layouts  33.6 us (12%)
  starting transfers between devices  30.5 us (11%)
  matrix products  24.5 us (8%)
  other arithmetic  16.2 us (6%)
  between operations  13.8 us (5%)
    all_gather x1, waiting for transfers between devices, in_one_piece(): lax.all_gather(both, axis, axis=dim, tiled=True)  84 us
    all_gather x1, waiting for transfers between devices, local(): features = lax.all_gather(chosen, 'tp', axis=1, tiled=True)  66.6 us
    dot_general x2, matrix products, local(): jnp.dot(normed, weight_rows, preferred_element_type=jnp.float32)  11.7 us
    ppermute x3, starting transfers between devices, from_partner(): return lax.ppermute(value, axis, pairs)  10.5 us
    all_to_all x1, waiting for transfers between devices, local(): lax.all_to_all(mixed_rows, 'grp', split_axis=0, concat_axis=0, tiled=True)  9.94 us
    sub x1, matrix products, local(): powered = jnp.exp(scores - row_max)  8.28 us
    all_to_all x1, starting transfers between devices, local(): lax.all_to_all(place_send, 'grp', split_axis=0, concat_axis=0, tiled=True)  7.58 us
  transfers between devices with their start and end apart: 9, of which 6 were waited for; matrix products, arithmetic and copies ran while one was open for 14% of the time, Pallas kernels for 0%

commit v1 on v0

v1 whole, which is shorter than its diff:
```python
import functools
import math

import jax
import jax.numpy as jnp
from jax import lax
from jax.experimental import pallas as pl
from jax.experimental.pallas import tpu as pltpu
from jax.sharding import PartitionSpec as P

HD = 128
EPS = 1e-05
MASKED = -1e30
LIFT = 64.0
MIB = 2**20
BF16, F32, I32 = jnp.bfloat16, jnp.float32, jnp.int32
VMEM = pl.BlockSpec(memory_space=pltpu.VMEM)
ANY = pl.BlockSpec(memory_space=pl.ANY)


def iota(shape, dim):
    return lax.broadcasted_iota(I32, shape, dim)


def ones_where(mask):
    return jnp.where(mask, 1.0, 0.0).astype(BF16)


def dot(a, b):
    return jnp.dot(a, b, preferred_element_type=F32)


def dot_nt(a, b):
    return lax.dot_general(a, b, (((1,), (1,)), ((), ())), preferred_element_type=F32)


def fold(parts):
    return functools.reduce(lambda a, b: a + b, parts)


def split_number(value):
    high = lax.shift_right_logical(value, 5)
    return high.astype(F32), (value - 32 * high).astype(F32)


def stack_rows(rows):
    shape = (8, rows[0].shape[1])
    at = iota(shape, 0)
    return fold(jnp.where(at == k, row, 0.0) for k, row in enumerate(rows)).astype(BF16)


def prepare_kernel(
    groups, pair_heads, modality_ref, owner_ref, doc_ref, token_ref, query_ref, pair_ref,
    chosen_ref, info_ref, packed_ref, spread_ref, block, sems,
):
    tok = token_ref.shape[0]
    half = chosen_ref.shape[0]
    slots = tok // groups
    rows, head_cols = query_ref.shape[1:]
    cols = head_cols + HD
    tower = lax.axis_index("tower")
    rank = lax.axis_index("tp")
    per_head = lax.axis_size("tp") // pair_heads
    column = (rank // per_head) * 2 * HD + (rank % 2) * HD
    loads = (
        pltpu.make_async_copy(
            query_ref.at[0], block.at[pl.ds(0, rows), pl.ds(0, head_cols)], sems.at[2 * groups]
        ),
        pltpu.make_async_copy(
            pair_ref.at[0, :, pl.ds(pl.multiple_of(column, HD), HD)],
            block.at[pl.ds(0, rows), pl.ds(head_cols, HD)],
            sems.at[2 * groups + 1],
        ),
    )
    for copy in loads:
        copy.start()
    for copy in loads:
        copy.wait()
    weights = [
        pltpu.make_async_copy(
            block.at[pl.ds(0, rows)], spread_ref.at[g, pl.ds(0, rows)], sems.at[g]
        )
        for g in range(groups)
    ]
    for copy in weights:
        copy.start()

    modality, owner = modality_ref[...], owner_ref[...]
    match = iota((groups, tok), 0) == owner
    text = jnp.where(match & (modality == 0), 1.0, 0.0)
    image = jnp.where(match & (modality == 1), 1.0, 0.0)
    both = jnp.concatenate([text, image], axis=0)
    before = ones_where(iota((tok, tok), 0) < iota((tok, tok), 1))
    counts = dot(both.astype(BF16), before)
    in_owner = counts * both
    text_slot = jnp.sum(in_owner[:groups], axis=0, keepdims=True)
    image_slot = (slots - 1.0) - jnp.sum(in_owner[groups:], axis=0, keepdims=True)
    slot = jnp.where(modality == 1, image_slot, text_slot).astype(I32)
    dest = owner * slots + slot
    text_rank = jnp.sum(counts[:groups], axis=0, keepdims=True)
    image_rank = jnp.sum(counts[groups:], axis=0, keepdims=True)
    in_tower = modality == tower
    own_rank = jnp.where(modality == 1, image_rank, text_rank).astype(I32)
    own_rank = jnp.where(in_tower, own_rank, half)
    select = ones_where(iota((half, tok), 0) == own_rank)
    chosen_ref[...] = dot(select, token_ref[...]).astype(BF16)

    at = iota((8, tok), 0)
    info_ref[...] = jnp.where(at == 0, dest, jnp.where(at == 1, in_tower.astype(I32), 0))
    high, low = split_number(dest)
    packed = dot_nt(stack_rows([high, low]), select)
    packed_ref[...] = (32.0 * packed[0:1] + packed[1:2]).astype(I32) + iota((8, half), 0) * 0

    high, low = split_number(iota((1, tok), 1))
    facts = stack_rows([doc_ref[...].astype(F32), high, low, modality.astype(F32)])
    table = dot_nt(facts, ones_where(iota((tok, tok), 0) == dest))
    if tok < cols:
        table = jnp.concatenate([table, jnp.zeros((8, 2 * cols - tok), F32)], axis=1)
    block[rows : rows + 16, :] = jnp.concatenate(
        [table[:, :cols], table[:, cols:]], axis=0
    ).astype(BF16)
    notes = [
        pltpu.make_async_copy(
            block.at[pl.ds(rows, 16)], spread_ref.at[g, pl.ds(rows, 16)], sems.at[groups + g]
        )
        for g in range(groups)
    ]
    for copy in notes:
        copy.start()
    for copy in weights + notes:
        copy.wait()


def prepare(modality, owner_ids, doc_ids, tokens, query_weight, pair_weight, groups):
    tok, slab = tokens.shape
    rows, head_cols = query_weight.shape[1:]
    half, cols = tok // 2, head_cols + HD
    kernel = functools.partial(prepare_kernel, groups, pair_weight.shape[2] // (2 * HD))
    return pl.pallas_call(
        kernel,
        out_shape=(
            jax.ShapeDtypeStruct((half, slab), BF16),
            jax.ShapeDtypeStruct((8, tok), I32),
            jax.ShapeDtypeStruct((8, half), I32),
            jax.ShapeDtypeStruct((groups, rows + 16, cols), BF16),
        ),
        in_specs=[VMEM, VMEM, VMEM, VMEM, ANY, ANY],
        out_specs=(VMEM, VMEM, VMEM, ANY),
        scratch_shapes=[
            pltpu.VMEM((rows + 16, cols), BF16),
            pltpu.SemaphoreType.DMA((2 * groups + 2,)),
        ],
        compiler_params=pltpu.CompilerParams(vmem_limit_bytes=32 * MIB),
        name="prepare",
    )(modality[None], owner_ids[None], doc_ids[None], tokens, query_weight, pair_weight)


def project_kernel(width, feature_ref, weight_ref, gain_ref, query_ref, pair_ref, total, squares):
    step = pl.program_id(0)

    @pl.when(step == 0)
    def _():
        total[...] = jnp.zeros_like(total)
        squares[...] = jnp.zeros_like(squares)

    values = feature_ref[0].astype(F32)
    squared = values * values
    slab = values.shape[1]
    squares[...] += fold(squared[:, c : c + HD] for c in range(0, slab, HD))
    scaled = (values * gain_ref[...]).astype(BF16)
    total[...] += dot(scaled, weight_ref[0])

    @pl.when(step == pl.num_programs(0) - 1)
    def _():
        mean = jnp.sum(squares[...], axis=1, keepdims=True) * (1.0 / width)
        rows = total[...] * lax.rsqrt(mean + EPS)
        head_cols = query_ref.shape[1]
        query_ref[...] = rows[:, :head_cols].astype(BF16)
        pair_ref[...] = rows[:, head_cols:].astype(BF16)


def project(features, weights, gain):
    count, half, slab = features.shape
    groups, _, cols = weights.shape
    rows = weights.shape[1] - 16
    head_cols = cols - HD
    assert groups * rows == count * slab and rows == slab
    return pl.pallas_call(
        functools.partial(project_kernel, count * slab),
        grid=(count,),
        out_shape=(
            jax.ShapeDtypeStruct((half, head_cols), BF16),
            jax.ShapeDtypeStruct((half, HD), BF16),
        ),
        in_specs=[
            pl.BlockSpec((1, half, slab), lambda k: (k, 0, 0)),
            pl.BlockSpec((1, rows, cols), lambda k: (k, 0, 0)),
            pl.BlockSpec((1, slab), lambda k: (0, k)),
        ],
        out_specs=(
            pl.BlockSpec((half, head_cols), lambda k: (0, 0)),
            pl.BlockSpec((half, HD), lambda k: (0, 0)),
        ),
        scratch_shapes=[pltpu.VMEM((half, cols), F32), pltpu.VMEM((half, HD), F32)],
        compiler_params=pltpu.CompilerParams(vmem_limit_bytes=24 * MIB),
        name="project",
    )(features, weights, gain)


def place_kernel(packed_ref, query_ref, mine_ref, other_ref, out_ref):
    tok, half = out_ref.shape[1], query_ref.shape[0]
    place = ones_where(iota((tok, half), 0) == packed_ref[0:1, :])
    queries = dot(place, query_ref[...]).astype(BF16)
    mine = dot(place, mine_ref[...]).astype(BF16)
    other = dot(place, other_ref[...]).astype(BF16)
    for core in range(2):
        out_ref[core, :, :HD] = queries[:, core * HD : (core + 1) * HD]

    def pair(keys, values):
        for core in range(2):
            out_ref[core, :, HD : 2 * HD] = keys
            out_ref[core, :, 2 * HD :] = values

    even = lax.axis_index("tp") % 2 == 0

    @pl.when(even)
    def _():
        pair(mine, other)

    @pl.when(jnp.logical_not(even))
    def _():
        pair(other, mine)


def place(packed, query_rows, mine, other, tok):
    return pl.pallas_call(
        place_kernel,
        out_shape=jax.ShapeDtypeStruct((2, tok, 3 * HD), BF16),
        in_specs=[VMEM] * 4,
        out_specs=VMEM,
        compiler_params=pltpu.CompilerParams(vmem_limit_bytes=24 * MIB),
        name="place",
    )(packed, query_rows, mine, other)


def mask_kernel(tok, note_ref, info_ref, bias_ref, back_ref):
    groups, _, cols = note_ref.shape
    slots = tok // groups
    group = lax.axis_index("grp")
    notes = note_ref[...].astype(F32)
    facts = jnp.concatenate([notes[:, :8], notes[:, 8:]], axis=2)[:, :, :tok]
    facts = facts.reshape(groups * 8, tok).astype(BF16)

    def part(index):
        return jnp.floor((index.astype(F32) + 0.5) * (1.0 / slots))

    column = iota((1, tok), 1)
    from_group = part(column)
    slot = column - slots * from_group.astype(I32)
    take = ones_where(iota((tok, tok), 0) == group * slots + slot)
    seen = dot(facts, take).reshape(groups, 8, tok)
    at = iota((groups, 8, tok), 0)
    rows = jnp.sum(jnp.where(at == from_group.astype(I32)[None], seen, 0.0), axis=0)
    same = ones_where(iota((tok, tok), 0) == iota((tok, tok), 1))
    turned = dot_nt(same, rows.astype(BF16))
    row_place = tok * from_group + 32.0 * rows[1:2] + rows[2:3]
    turned_place = tok * part(iota((tok, 1), 0)) + 32.0 * turned[:, 1:2] + turned[:, 2:3]
    after = (row_place <= turned_place) | (rows[3:4] * turned[:, 3:4] > 0.5)
    allowed = (rows[0:1] == turned[:, 0:1]) & after
    bias_ref[...] = jnp.where(allowed, 0.0, MASKED).astype(BF16)

    high, low = split_number(info_ref[0:1, :])
    back = dot_nt(same, stack_rows([high, low, info_ref[1:2, :].astype(F32)]))
    dest = (32.0 * back[:, 0:1] + back[:, 1:2]).astype(I32)
    dest = jnp.where(back[:, 2:3] > 0.5, dest, -1)
    back_ref[...] = ones_where(iota((tok, tok), 1) == dest)


def masks(weights, info):
    tok = info.shape[1]
    groups, rows, cols = weights.shape
    at = rows // 16 - 1
    return pl.pallas_call(
        functools.partial(mask_kernel, tok),
        grid=(1,),
        out_shape=(
            jax.ShapeDtypeStruct((tok, tok), BF16),
            jax.ShapeDtypeStruct((tok, tok), BF16),
        ),
        in_specs=[
            pl.BlockSpec((groups, 16, cols), lambda k: (0, at, 0)),
            pl.BlockSpec((8, tok), lambda k: (0, 0)),
        ],
        out_specs=(
            pl.BlockSpec((tok, tok), lambda k: (0, 0)),
            pl.BlockSpec((tok, tok), lambda k: (0, 0)),
        ),
        compiler_params=pltpu.CompilerParams(vmem_limit_bytes=40 * MIB),
        name="masks",
    )(weights, info)


def attend_kernel(given_ref, bias_ref, out_ref):
    tok = given_ref.shape[1]
    merged = given_ref[0] + given_ref[1]
    keys, values = merged[:, HD : 2 * HD], merged[:, 2 * HD :]
    tile = min(256, tok)
    for at in range(0, tok, tile):
        scores = dot_nt(merged[at : at + tile, :HD], keys) * (1.0 / math.sqrt(HD))
        scores = scores + bias_ref[at : at + tile, :].astype(F32)
        powered = jnp.exp(scores - jnp.max(scores, axis=1, keepdims=True))
        inverse = 1.0 / jnp.sum(powered, axis=1, keepdims=True)
        mixed = dot((powered * inverse).astype(BF16), values).astype(BF16)
        out_ref[0, at : at + tile, :] = mixed
        out_ref[1, at : at + tile, :] = mixed


def attend(given, bias):
    tok = bias.shape[0]
    return pl.pallas_call(
        attend_kernel,
        out_shape=jax.ShapeDtypeStruct((2, tok, HD), BF16),
        in_specs=[VMEM, VMEM],
        out_specs=VMEM,
        compiler_params=pltpu.CompilerParams(vmem_limit_bytes=32 * MIB),
        name="attend",
    )(given, bias)


def restore_kernel(back_ref, given_ref, out_ref):
    for core in range(2):
        out_ref[0, :, core * HD : (core + 1) * HD] = dot(back_ref[...], given_ref[core]).astype(BF16)


def restore(back, given):
    tok = back.shape[0]
    return pl.pallas_call(
        restore_kernel,
        out_shape=jax.ShapeDtypeStruct((1, tok, 2 * HD), BF16),
        in_specs=[VMEM, VMEM],
        out_specs=VMEM,
        compiler_params=pltpu.CompilerParams(vmem_limit_bytes=24 * MIB),
        name="restore",
    )(back, given)


def swap_all(value, axes):
    return lax.all_to_all(value, axes, split_axis=0, concat_axis=0, tiled=True)


def local(tokens, modality, doc_ids, owner_ids, norm_gain, query_weight, pair_weight):
    groups = lax.axis_size("grp")
    tok = tokens.shape[0]
    slots = tok // groups
    chosen, info, packed, spread = prepare(
        modality, owner_ids, doc_ids, tokens, query_weight, pair_weight, groups
    )
    weights = swap_all(spread, "grp")
    lifted = (chosen.astype(F32) * LIFT).astype(jnp.float16)
    gathered = lax.all_gather(lifted, "tp", axis=0)
    features = (gathered.astype(F32) * (1.0 / LIFT)).astype(BF16)
    query_rows, mine = project(features, weights, norm_gain)
    pairs = [(t, t ^ 1) for t in range(lax.axis_size("tp"))]
    other = lax.ppermute(mine, "tp", pairs)
    sent = place(packed, query_rows, mine, other, tok)
    weights, info, sent = lax.optimization_barrier((weights, info, sent))
    given = swap_all(sent.reshape(2 * groups, slots, 3 * HD), ("tower", "grp"))
    bias, back = masks(weights, info)
    mixed = attend(given.reshape(2, tok, 3 * HD), bias)
    returned = swap_all(mixed.reshape(2 * groups, slots, HD), ("tower", "grp"))
    return restore(back, returned.reshape(2, tok, HD))


def solution(mesh):
    in_specs = (
        P("grp", "tp"),
        P("grp"),
        P("grp"),
        P("grp"),
        P("tower", None),
        P("tower", "grp", "tp"),
        P("tower", "grp", None),
    )
    out_specs = P("tower", "grp", "tp")
    return jax.shard_map(local, mesh=mesh, in_specs=in_specs, out_specs=out_specs, check_vma=False)
```

time: 290 us -> 183 us (0.63)
  waiting for transfers between devices: 171 us -> 22.6 us
  blocking collectives: 0 us -> 91.7 us
  Pallas kernels: 0 us -> 24.9 us
  matrix products: 24.5 us -> 0 us
  local copies, waits for them, and re-layouts: 33.6 us -> 12.2 us
  between operations: 13.8 us -> 0.09 us
  other arithmetic: 16.2 us -> 4.38 us
  starting transfers between devices: 30.5 us -> 26 us
    all_gather x2 -> x0, waiting for transfers between devices: 151 us -> none  [the longest x1 84 us: in_one_piece(): lax.all_gather(both, axis, axis=dim, tiled=True)]
    all_gather x0 -> x1, blocking collectives: none -> 77.8 us  [local(): gathered = lax.all_gather(lifted, 'tp', axis=0)]
    pallas_call x0 -> x6, Pallas kernels: none -> 24.9 us  [the longest x1 11.9 us: project(): pl.pallas_call(functools.partial(project_kernel, count * slab), grid=(cou...]
    gather x6 -> x0, local copies, waits for them, and re-layouts: 20 us -> none  [the longest x1 5.01 us: local(): token_row = row_index[safe_row]]
    dot_general x3 -> x0, matrix products: 16.2 us -> none  [the longest x2 11.7 us: local(): jnp.dot(normed, weight_rows, preferred_element_type=jnp.float32)]
    all_to_all x0 -> x1, blocking collectives: none -> 13.9 us  [swap_all(): return lax.all_to_all(value, axes, split_axis=0, concat_axis=0, tiled=True)]
    unnamed x6 -> x16, local copies, waits for them, and re-layouts: 0.01 us -> 10.1 us
    sub x1 -> x0, matrix products: 8.28 us -> none  [local(): powered = jnp.exp(scores - row_max)]
  transfers between devices with their start and end apart: 9 -> 3, of which waited for: 6 -> 3; matrix products, arithmetic and copies ran while one was open for 14% -> 2% of each run, Pallas kernels for 0% -> 2%
where the time goes in v1:
time: 183 us; the launch traced here: 182 us
  blocking collectives  91.7 us (50%)
  starting transfers between devices  26 us (14%)
  Pallas kernels  24.9 us (14%)
  waiting for transfers between devices  22.6 us (12%)
  local copies, waits for them, and re-layouts  12.2 us (7%)
  other arithmetic  4.38 us (2%)
    all_gather x1, blocking collectives, local(): gathered = lax.all_gather(lifted, 'tp', axis=0)  77.8 us
    all_to_all x2, waiting for transfers between devices, swap_all(): return lax.all_to_all(value, axes, split_axis=0, concat_axis=0, tiled=True)  20.6 us
    all_to_all x2, starting transfers between devices, swap_all(): return lax.all_to_all(value, axes, split_axis=0, concat_axis=0, tiled=True)  16 us
    all_to_all x1, blocking collectives, swap_all(): return lax.all_to_all(value, axes, split_axis=0, concat_axis=0, tiled=True)  13.9 us
    pallas_call x1, Pallas kernels, project(): pl.pallas_call(functools.partial(project_kernel, count * slab), grid=(cou...  11.9 us
    unnamed x16, local copies, waits for them, and re-layouts  10.1 us
    ppermute x1, starting transfers between devices, local(): other = lax.ppermute(mine, 'tp', pairs)  10 us
    pallas_call x1, Pallas kernels, prepare(): pl.pallas_call(kernel, out_shape=(jax.ShapeDtypeStruct((half, slab), BF16...  4.81 us
  transfers between devices with their start and end apart: 3, of which 3 were waited for; matrix products, arithmetic and copies ran while one was open for 2% of the time, Pallas kernels for 2%

profile of v1, /device:TPU:1, one launch (start us, length us, event | category | flops | bytes accessed | tf_op | source)
XLA Modules:
  0.0 181.9 jit_solution(17248527319880786576)
XLA Ops:
  0.0 0.7 broadcast_in_dim.9.modality_ref
  0.7 0.7 broadcast_in_dim.11.doc_ref
  1.4 0.7 broadcast_in_dim.10.owner_ref
  2.1 1.2 copy-done.2
  3.3 1.1 copy-done.3
  4.4 0.9 copy-done.4
  5.4 4.8 %prepare.1 = (bf16[384,512]{1,0:T(8,128)(2,1)S(1)}, s32[8,768]{1,0:T(8,128)S(1)}, s32[8,384]{1,0:T(8,128)S(1)}, bf16[16,528,384]{2,1,0:T(8,128)(2,1)S(1)}) custom-call(s32[1,768]{1,0:T(1,128)S(1)} %broadcast_in_dim.9.modality_ref, s32[1,768]{1,0:T(1,128)S(1)} %broadcast_in_dim.10.owner_ref, s32[1,768]{1,0:T(1,128)S(1)} %broadcast_in_dim.11.doc_ref, ...), custom_call_target="tpu_custom_call" | custom-call | tf_op jit(solution)/shard_map/prepare/pallas_call | solution.py:139
  10.2 2.7 %copy-done.1 = bf16[16,528,384]{2,1,0:T(8,128)(2,1)} copy-done((bf16[16,528,384]{2,1,0:T(8,128)(2,1)}, bf16[16,528,384]{2,1,0:T(8,128)(2,1)S(1)}, u32[]{:S(2)}) %copy-start.1) | copy-done | bytes 6488088
  13.5 7.6 %all-to-all-start = ((bf16[16,528,384]{2,1,0:T(8,128)(2,1)}), bf16[16,528,384]{2,1,0:T(8,128)(2,1)}, u32[]{:S(2)}, u32[]{:S(2)}) async-start(bf16[16,528,384]{2,1,0:T(8,128)(2,1)} %copy-done.1), calls=%async_computation | async-start | bytes 12976128 | tf_op jit(solution)/shard_map/all_to_all | solution.py:348
  21.2 77.8 %all-gather.2 = f16[6144,512]{1,0:T(8,128)(2,1)S(1)} all-gather(f16[384,512]{1,0:T(8,128)(2,1)S(1)} %multiply_convert_fusion.1), channel_id=2, replica_groups=mesh['tower'=2,'tp'=16,'grp'=16] {'tp'}, dimensions={0}, use_global_device_ids=true | all-gather | bytes 6684672 | tf_op jit(solution)/shard_map/all_gather | solution.py:360
  99.1 4.3 %multiply_convert_fusion = bf16[6144,512]{1,0:T(8,128)(2,1)} fusion(f16[6144,512]{1,0:T(8,128)(2,1)S(1)} %all-gather.2), kind=kLoop, calls=%fused_computation | loop fusion | flops 9437184 | bytes 12582912 | tf_op jit(solution)/shard_map/convert_element_type | solution.py:361
  103.4 6.5 %all-to-all-done.weight_ref.note_ref = bf16[16,528,384]{2,1,0:T(8,128)(2,1)} async-done(((bf16[16,528,384]{2,1,0:T(8,128)(2,1)}), bf16[16,528,384]{2,1,0:T(8,128)(2,1)}, u32[]{:S(2)}, u32[]{:S(2)}) %all-to-all-start) | async-done | bytes 6488096 | tf_op jit(solution)/shard_map/all_to_all | solution.py:348
  109.9 2.8 %copy-done = bf16[6144,512]{1,0:T(8,128)(2,1)S(1)} copy-done((bf16[6144,512]{1,0:T(8,128)(2,1)S(1)}, bf16[6144,512]{1,0:T(8,128)(2,1)}, u32[]{:S(2)}) %copy-start) | copy-done | bytes 6291480
  112.7 11.9 %project.1 = (bf16[384,256]{1,0:T(8,128)(2,1)S(1)}, bf16[384,128]{1,0:T(8,128)(2,1)S(1)}) custom-call(bf16[16,384,512]{2,1,0:T(8,128)(2,1)S(1)} %bitcast.5, bf16[16,528,384]{2,1,0:T(8,128)(2,1)} %all-to-all-done.weight_ref.note_ref, f32[1,8192]{1,0:T(1,128)S(1)} %copy-done.5), custom_call_target="tpu_custom_call" | custom-call | tf_op jit(solution)/shard_map/project/pallas_call | solution.py:188
  124.6 10.0 %collective-permute-start = (bf16[384,128]{1,0:T(8,128)(2,1)S(1)}, bf16[384,128]{1,0:T(8,128)(2,1)S(1)}, u32[]{:S(2)}, u32[]{:S(2)}) collective-permute-start(bf16[384,128]{1,0:T(8,128)(2,1)S(1)} %get-tuple-element.21.mine_ref), channel_id=1, source_target_pairs={{0,16},{16,0},{32,48},{48,32},{64,80},{80,64},{96,112},{112,96},{1... | collective-permute-start | bytes 294920 | tf_op jit(solution)/shard_map/ppermute | solution.py:364
  134.6 2.0 %collective-permute-done.other_ref = bf16[384,128]{1,0:T(8,128)(2,1)S(1)} collective-permute-done((bf16[384,128]{1,0:T(8,128)(2,1)S(1)}, bf16[384,128]{1,0:T(8,128)(2,1)S(1)}, u32[]{:S(2)}, u32[]{:S(2)}) %collective-permute-start) | collective-permute-done | bytes 98336 | tf_op jit(solution)/shard_map/ppermute | solution.py:364
  136.6 1.8 place.1
  138.4 8.4 %all-to-all-start.1 = ((bf16[32,48,384]{2,1,0:T(8,128)(2,1)}), bf16[32,48,384]{2,1,0:T(8,128)(2,1)S(1)}, u32[]{:S(2)}, u32[]{:S(2)}) async-start(bf16[32,48,384]{2,1,0:T(8,128)(2,1)} %bitcast.1), calls=%async_computation.1 | async-start | bytes 2359296 | tf_op jit(solution)/shard_map/all_to_all | solution.py:348
  146.8 0.7 copy-done.7
  147.6 3.1 %masks.1 = (bf16[768,768]{1,0:T(8,128)(2,1)S(1)}, bf16[768,768]{1,0:T(8,128)(2,1)S(1)}) custom-call(bf16[16,528,384]{2,1,0:T(8,128)(2,1)} %all-to-all-done.weight_ref.note_ref, s32[8,768]{1,0:T(8,128)S(1)} %copy-done.7), custom_call_target="tpu_custom_call" | custom-call | tf_op jit(solution)/shard_map/masks/pallas_call | solution.py:283
  150.7 14.1 %all-to-all-done.1 = bf16[32,48,384]{2,1,0:T(8,128)(2,1)S(1)} async-done(((bf16[32,48,384]{2,1,0:T(8,128)(2,1)}), bf16[32,48,384]{2,1,0:T(8,128)(2,1)S(1)}, u32[]{:S(2)}, u32[]{:S(2)}) %all-to-all-start.1) | async-done | bytes 1179680 | tf_op jit(solution)/shard_map/all_to_all | solution.py:348
  164.7 1.8 attend.1
  166.5 13.9 %all_to_all.15 = bf16[32,48,128]{2,1,0:T(8,128)(2,1)S(1)} all-to-all(bf16[32,48,128]{2,1,0:T(8,128)(2,1)S(1)} %bitcast.8), channel_id=1, replica_groups=mesh['tower'=2,'tp'=16,'grp'=16] {'tower','grp'}, dimensions={0} | all-to-all | bytes 786432 | tf_op jit(solution)/shard_map/all_to_all | solution.py:348
  180.4 1.5 restore.1
  (11 shorter events, 0.7 us)
Async XLA Ops:
  2.1 1.2 copy-start.2
  3.3 1.1 copy-start.3
  4.4 0.9 copy-start.4
  10.2 2.7 %copy-start.1 = (bf16[16,528,384]{2,1,0:T(8,128)(2,1)}, bf16[16,528,384]{2,1,0:T(8,128)(2,1)S(1)}, u32[]{:S(2)}) copy-start(bf16[16,528,384]{2,1,0:T(8,128)(2,1)S(1)} %get-tuple-element.16) | copy-start | bytes 19464196
  12.9 0.6 copy-start.6
  13.5 96.4 %all-to-all-start = ((bf16[16,528,384]{2,1,0:T(8,128)(2,1)}), bf16[16,528,384]{2,1,0:T(8,128)(2,1)}, u32[]{:S(2)}, u32[]{:S(2)}) async-start(bf16[16,528,384]{2,1,0:T(8,128)(2,1)} %copy-done.1), calls=%async_computation | async-start | bytes 12976128 | tf_op jit(solution)/shard_map/all_to_all | solution.py:348
  99.1 10.8 %copy-start.5 = (f32[1,8192]{1,0:T(1,128)S(1)}, f32[1,8192]{1,0:T(1,128)}, u32[]{:S(2)}) copy-start(f32[1,8192]{1,0:T(1,128)} %gain_ref.1) | copy-start | bytes 98308
  109.9 2.8 %copy-start = (bf16[6144,512]{1,0:T(8,128)(2,1)S(1)}, bf16[6144,512]{1,0:T(8,128)(2,1)}, u32[]{:S(2)}) copy-start(bf16[6144,512]{1,0:T(8,128)(2,1)} %multiply_convert_fusion) | copy-start | bytes 18874372
  124.6 12.0 %collective-permute-start = (bf16[384,128]{1,0:T(8,128)(2,1)S(1)}, bf16[384,128]{1,0:T(8,128)(2,1)S(1)}, u32[]{:S(2)}, u32[]{:S(2)}) collective-permute-start(bf16[384,128]{1,0:T(8,128)(2,1)S(1)} %get-tuple-element.21.mine_ref), channel_id=1, source_target_pairs={{0,16},{16,0},{32,48},{48,32},{64,80},{80,64},{96,112},{112,96},{1... | collective-permute-start | bytes 294920 | tf_op jit(solution)/shard_map/ppermute | solution.py:364
  138.4 26.3 %all-to-all-start.1 = ((bf16[32,48,384]{2,1,0:T(8,128)(2,1)}), bf16[32,48,384]{2,1,0:T(8,128)(2,1)S(1)}, u32[]{:S(2)}, u32[]{:S(2)}) async-start(bf16[32,48,384]{2,1,0:T(8,128)(2,1)} %bitcast.1), calls=%async_computation.1 | async-start | bytes 2359296 | tf_op jit(solution)/shard_map/all_to_all | solution.py:348
  146.8 0.7 copy-start.7

commit v2 on v1

v2 whole, which is shorter than its diff:
```python
import functools
import math

import jax
import jax.numpy as jnp
from jax import lax
from jax.experimental import pallas as pl
from jax.experimental.pallas import tpu as pltpu
from jax.sharding import PartitionSpec as P

HD = 128
EPS = 1e-05
MASKED = -1e30
LIFT = 64.0
MIB = 2**20
BF16, F32, I32 = jnp.bfloat16, jnp.float32, jnp.int32
VMEM = pl.BlockSpec(memory_space=pltpu.VMEM)
HBM = pl.BlockSpec(memory_space=pltpu.HBM)


def iota(shape, dim):
    return lax.broadcasted_iota(I32, shape, dim)


def ones_where(mask):
    return jnp.where(mask, 1.0, 0.0).astype(BF16)


def dot(a, b):
    return jnp.dot(a, b, preferred_element_type=F32)


def dot_nt(a, b):
    return lax.dot_general(a, b, (((1,), (1,)), ((), ())), preferred_element_type=F32)


def fold(parts):
    return functools.reduce(lambda a, b: a + b, parts)


def split_number(value):
    high = lax.shift_right_logical(value, 5)
    return high.astype(F32), (value - 32 * high).astype(F32)


def stack_rows(rows):
    shape = (8, rows[0].shape[1])
    at = iota(shape, 0)
    return fold(jnp.where(at == k, row, 0.0) for k, row in enumerate(rows)).astype(BF16)


def slots_of(modality, owner, groups):
    tok = owner.shape[1]
    slots = tok // groups
    match = iota((groups, tok), 0) == owner
    text = jnp.where(match & (modality == 0), 1.0, 0.0)
    image = jnp.where(match & (modality == 1), 1.0, 0.0)
    both = jnp.concatenate([text, image], axis=0)
    before = ones_where(iota((tok, tok), 0) < iota((tok, tok), 1))
    counts = dot(both.astype(BF16), before)
    in_owner = counts * both
    text_slot = jnp.sum(in_owner[:groups], axis=0, keepdims=True)
    image_slot = (slots - 1.0) - jnp.sum(in_owner[groups:], axis=0, keepdims=True)
    slot = jnp.where(modality == 1, image_slot, text_slot).astype(I32)
    text_rank = jnp.sum(counts[:groups], axis=0, keepdims=True)
    image_rank = jnp.sum(counts[groups:], axis=0, keepdims=True)
    rank = jnp.where(modality == 1, image_rank, text_rank).astype(I32)
    return owner * slots + slot, rank


def row_of(ref):
    return ref[...].reshape(1, ref.shape[0])


def in_hbm(*arrays):
    return tuple(pltpu.with_memory_space_constraint(a, pltpu.HBM) for a in arrays)


def pack_kernel(
    groups, pair_heads, modality_ref, owner_ref, doc_ref, query_ref, pair_ref,
    spread_ref, block, modality_own, owner_own, doc_own, sems,
):
    tok = modality_ref.shape[0]
    rows, head_cols = query_ref.shape[1:]
    cols = head_cols + HD
    rank = lax.axis_index("tp")
    per_head = lax.axis_size("tp") // pair_heads
    column = (rank // per_head) * 2 * HD + (rank % 2) * HD
    sources = (
        (query_ref.at[0], block.at[pl.ds(0, rows), pl.ds(0, head_cols)]),
        (
            pair_ref.at[0, :, pl.ds(pl.multiple_of(column, HD), HD)],
            block.at[pl.ds(0, rows), pl.ds(head_cols, HD)],
        ),
        (modality_ref, modality_own),
        (owner_ref, owner_own),
        (doc_ref, doc_own),
    )
    loads = [
        pltpu.make_async_copy(source, target, sems.at[2 * groups + k])
        for k, (source, target) in enumerate(sources)
    ]
    for copy in loads:
        copy.start()
    for copy in loads[:2]:
        copy.wait()
    weights = [
        pltpu.make_async_copy(
            block.at[pl.ds(0, rows)], spread_ref.at[g, pl.ds(0, rows)], sems.at[g]
        )
        for g in range(groups)
    ]
    for copy in weights:
        copy.start()
    for copy in loads[2:]:
        copy.wait()
    modality = row_of(modality_own)
    dest, _ = slots_of(modality, row_of(owner_own), groups)
    high, low = split_number(iota((1, tok), 1))
    facts = stack_rows([row_of(doc_own).astype(F32), high, low, modality.astype(F32)])
    table = dot_nt(facts, ones_where(iota((tok, tok), 0) == dest))
    if tok < 2 * cols:
        table = jnp.concatenate([table, jnp.zeros((8, 2 * cols - tok), F32)], axis=1)
    block[rows : rows + 16, :] = jnp.concatenate(
        [table[:, :cols], table[:, cols:]], axis=0
    ).astype(BF16)
    notes = [
        pltpu.make_async_copy(
            block.at[pl.ds(rows, 16)], spread_ref.at[g, pl.ds(rows, 16)], sems.at[groups + g]
        )
        for g in range(groups)
    ]
    for copy in notes:
        copy.start()
    for copy in weights + notes:
        copy.wait()


def pack(modality, owner_ids, doc_ids, query_weight, pair_weight, groups):
    tok = modality.shape[0]
    rows, head_cols = query_weight.shape[1:]
    cols = head_cols + HD
    kernel = functools.partial(pack_kernel, groups, pair_weight.shape[2] // (2 * HD))
    return pl.pallas_call(
        kernel,
        out_shape=pltpu.HBM((groups, rows + 16, cols), BF16),
        in_specs=[HBM] * 5,
        out_specs=HBM,
        scratch_shapes=[
            pltpu.VMEM((rows + 16, cols), BF16),
            pltpu.VMEM((tok,), I32),
            pltpu.VMEM((tok,), I32),
            pltpu.VMEM((tok,), I32),
            pltpu.SemaphoreType.DMA((2 * groups + 5,)),
        ],
        compiler_params=pltpu.CompilerParams(vmem_limit_bytes=16 * MIB),
        name="pack",
    )(*in_hbm(modality, owner_ids, doc_ids, query_weight, pair_weight))


def choose_kernel(modality_ref, token_ref, chosen_ref, modality_own, token_own, sems):
    tok, half = token_ref.shape[0], chosen_ref.shape[0]
    loads = (
        pltpu.make_async_copy(modality_ref, modality_own, sems.at[0]),
        pltpu.make_async_copy(token_ref, token_own, sems.at[1]),
    )
    for copy in loads:
        copy.start()
    loads[0].wait()
    mine = row_of(modality_own) == lax.axis_index("tower")
    before = ones_where(iota((tok, tok), 0) < iota((tok, tok), 1))
    flags = jnp.broadcast_to(jnp.where(mine, 1.0, 0.0), (8, tok)).astype(BF16)
    rank = jnp.where(mine, dot(flags, before)[0:1].astype(I32), half)
    select = ones_where(iota((half, tok), 0) == rank)
    loads[1].wait()
    chosen_ref[...] = dot(select, token_own[...]).astype(BF16)


def choose(modality, tokens):
    tok, slab = tokens.shape
    return pl.pallas_call(
        choose_kernel,
        out_shape=jax.ShapeDtypeStruct((tok // 2, slab), BF16),
        in_specs=[HBM, HBM],
        out_specs=VMEM,
        scratch_shapes=[
            pltpu.VMEM((tok,), I32),
            pltpu.VMEM((tok, slab), BF16),
            pltpu.SemaphoreType.DMA((2,)),
        ],
        compiler_params=pltpu.CompilerParams(vmem_limit_bytes=16 * MIB),
        name="choose",
    )(*in_hbm(modality, tokens))


def normalize_kernel(feature_ref, gain_ref, out_ref):
    count, half, slab = feature_ref.shape
    tile = 48 if half % 48 == 0 else 16

    @pl.loop(0, half // tile)
    def _(step):
        at = pl.ds(pl.multiple_of(step * tile, 16), tile)
        squares = jnp.zeros((tile, HD), F32)
        for k in range(count):
            values = feature_ref[k, at, :].astype(F32)
            squared = values * values
            squares += fold([squared[:, c : c + HD] for c in range(0, slab, HD)])
        mean = jnp.sum(squares, axis=1, keepdims=True) * (1.0 / (count * slab))
        inverse = lax.rsqrt(mean + EPS)
        for k in range(count):
            values = feature_ref[k, at, :].astype(F32) * inverse
            gain = gain_ref[:, k * slab : (k + 1) * slab]
            out_ref[k, at, :] = (values * gain).astype(BF16)


def normalize(features, gain):
    return pl.pallas_call(
        normalize_kernel,
        out_shape=jax.ShapeDtypeStruct(features.shape, BF16),
        in_specs=[VMEM, VMEM],
        out_specs=VMEM,
        compiler_params=pltpu.CompilerParams(vmem_limit_bytes=20 * MIB),
        name="normalize",
    )(features, gain)


def project_kernel(normed_ref, weight_ref, keep_ref, mine_ref, give_ref, rows, block, sems):
    count, _, slab = normed_ref.shape
    loads = []
    for k in range(count):
        loads.append(
            (
                pltpu.make_async_copy(normed_ref.at[k], rows.at[k], sems.at[2 * k]),
                pltpu.make_async_copy(
                    weight_ref.at[k, pl.ds(0, slab)], block.at[k], sems.at[2 * k + 1]
                ),
            )
        )
    for pair in loads:
        for copy in pair:
            copy.start()
    total = None
    together = 2
    for at in range(0, count, together):
        for pair in loads[at : at + together]:
            for copy in pair:
                copy.wait()
        term = fold([dot(rows[k], block[k]) for k in range(at, at + together)])
        total = term if total is None else total + term
    total = total.astype(BF16)
    mine = total[:, 2 * HD :]
    mine_ref[...] = mine
    give_ref[:, HD:] = mine
    text = lax.axis_index("tower") == 0

    @pl.when(text)
    def _():
        keep_ref[...] = total[:, :HD]
        give_ref[:, :HD] = total[:, HD : 2 * HD]

    @pl.when(jnp.logical_not(text))
    def _():
        keep_ref[...] = total[:, HD : 2 * HD]
        give_ref[:, :HD] = total[:, :HD]


def project(normed, weights):
    count, half, slab = normed.shape
    groups, rows, cols = weights.shape
    assert groups == count and rows == slab + 16 and cols == 3 * HD
    return pl.pallas_call(
        project_kernel,
        out_shape=(
            jax.ShapeDtypeStruct((half, HD), BF16),
            jax.ShapeDtypeStruct((half, HD), BF16),
            jax.ShapeDtypeStruct((half, 2 * HD), BF16),
        ),
        in_specs=[HBM, HBM],
        out_specs=(VMEM,) * 3,
        scratch_shapes=[
            pltpu.VMEM((count, half, slab), BF16),
            pltpu.VMEM((count, slab, cols), BF16),
            pltpu.SemaphoreType.DMA((2 * count,)),
        ],
        compiler_params=pltpu.CompilerParams(vmem_limit_bytes=32 * MIB),
        name="project",
    )(*in_hbm(normed, weights))


def plan_kernel(groups, modality_ref, owner_ref, place_ref):
    tok = place_ref.shape[0]
    half = tok // 2
    modality = row_of(modality_ref)
    dest, rank = slots_of(modality, row_of(owner_ref), groups)
    rank = jnp.where(modality == lax.axis_index("tower"), rank, half + rank)
    select = ones_where(iota((tok, tok), 0) == rank)
    high, low = split_number(dest)
    packed = dot_nt(stack_rows([high, low]), select)
    packed = (32.0 * packed[0:1] + packed[1:2]).astype(I32)
    place_ref[...] = ones_where(iota((tok, tok), 0) == packed)


def plan(modality, owner_ids, groups):
    tok = modality.shape[0]
    return pl.pallas_call(
        functools.partial(plan_kernel, groups),
        out_shape=jax.ShapeDtypeStruct((tok, tok), BF16),
        in_specs=[VMEM, VMEM],
        out_specs=VMEM,
        compiler_params=pltpu.CompilerParams(vmem_limit_bytes=24 * MIB),
        name="plan",
    )(modality, owner_ids)


def place_kernel(place_ref, keep_ref, got_ref, mine_ref, out_ref):
    half = keep_ref.shape[0]
    own, other = place_ref[:, :half], place_ref[:, half:]
    out_ref[:, :HD] = (dot(own, keep_ref[...]) + dot(other, got_ref[:, :HD])).astype(BF16)
    out_ref[:, HD:] = (dot(own, mine_ref[...]) + dot(other, got_ref[:, HD:])).astype(BF16)


def place(where, keep, got, mine):
    tok = where.shape[0]
    return pl.pallas_call(
        place_kernel,
        out_shape=jax.ShapeDtypeStruct((tok, 2 * HD), BF16),
        in_specs=[VMEM] * 4,
        out_specs=VMEM,
        compiler_params=pltpu.CompilerParams(vmem_limit_bytes=16 * MIB),
        name="place",
    )(where, keep, got, mine)


def mask_kernel(note_ref, modality_ref, owner_ref, bias_ref, back_ref, notes, sem):
    groups, rows, cols = note_ref.shape
    tok = bias_ref.shape[0]
    slots = tok // groups
    copy = pltpu.make_async_copy(note_ref.at[:, pl.ds(rows - 16, 16)], notes, sem)
    copy.start()
    modality = row_of(modality_ref)
    dest, _ = slots_of(modality, row_of(owner_ref), groups)
    same = ones_where(iota((tok, tok), 0) == iota((tok, tok), 1))
    high, low = split_number(dest)
    mine = jnp.where(modality == lax.axis_index("tower"), 1.0, 0.0)
    back = dot_nt(same, stack_rows([high, low, mine]))
    dest = (32.0 * back[:, 0:1] + back[:, 1:2]).astype(I32)
    dest = jnp.where(back[:, 2:3] > 0.5, dest, -1)
    back_ref[...] = ones_where(iota((tok, tok), 1) == dest)

    copy.wait()
    group = lax.axis_index("grp")
    seen = notes[...].astype(F32)
    facts = jnp.concatenate([seen[:, :8], seen[:, 8:]], axis=2)[:, :, :tok]
    facts = facts.reshape(groups * 8, tok).astype(BF16)

    def part(index):
        return jnp.floor((index.astype(F32) + 0.5) * (1.0 / slots))

    column = iota((1, tok), 1)
    from_group = part(column)
    slot = column - slots * from_group.astype(I32)
    take = ones_where(iota((tok, tok), 0) == group * slots + slot)
    seen = dot(facts, take).reshape(groups, 8, tok)
    at = iota((groups, 8, tok), 0)
    row = jnp.sum(jnp.where(at == from_group.astype(I32)[None], seen, 0.0), axis=0)
    turned = dot_nt(same, row.astype(BF16))
    row_place = tok * from_group + 32.0 * row[1:2] + row[2:3]
    turned_place = tok * part(iota((tok, 1), 0)) + 32.0 * turned[:, 1:2] + turned[:, 2:3]
    after = (row_place <= turned_place) | (row[3:4] * turned[:, 3:4] > 0.5)
    allowed = (row[0:1] == turned[:, 0:1]) & after
    bias_ref[...] = jnp.where(allowed, 0.0, MASKED).astype(BF16)


def masks(weights, modality, owner_ids):
    tok = modality.shape[0]
    groups, _, cols = weights.shape
    return pl.pallas_call(
        mask_kernel,
        out_shape=(
            jax.ShapeDtypeStruct((tok, tok), BF16),
            jax.ShapeDtypeStruct((tok, tok), BF16),
        ),
        in_specs=[HBM, VMEM, VMEM],
        out_specs=(VMEM, VMEM),
        scratch_shapes=[pltpu.VMEM((groups, 16, cols), BF16), pltpu.SemaphoreType.DMA],
        compiler_params=pltpu.CompilerParams(vmem_limit_bytes=32 * MIB),
        name="masks",
    )(*in_hbm(weights), modality, owner_ids)


def attend_kernel(given_ref, near_ref, bias_ref, out_ref):
    tok = given_ref.shape[0]
    mine = given_ref[:, HD:]
    tile = min(256, tok)

    def run(keys, values):
        for at in range(0, tok, tile):
            scores = dot_nt(given_ref[at : at + tile, :HD], keys) * (1.0 / math.sqrt(HD))
            scores = scores + bias_ref[at : at + tile, :].astype(F32)
            powered = jnp.exp(scores - jnp.max(scores, axis=1, keepdims=True))
            inverse = 1.0 / jnp.sum(powered, axis=1, keepdims=True)
            mixed = dot((powered * inverse).astype(BF16), values).astype(BF16)
            out_ref[0, at : at + tile, :] = mixed
            out_ref[1, at : at + tile, :] = mixed

    even = lax.axis_index("tp") % 2 == 0

    @pl.when(even)
    def _():
        run(mine, near_ref[...])

    @pl.when(jnp.logical_not(even))
    def _():
        run(near_ref[...], mine)


def attend(given, near, bias):
    tok = bias.shape[0]
    return pl.pallas_call(
        attend_kernel,
        out_shape=jax.ShapeDtypeStruct((2, tok, HD), BF16),
        in_specs=[VMEM] * 3,
        out_specs=VMEM,
        compiler_params=pltpu.CompilerParams(vmem_limit_bytes=24 * MIB),
        name="attend",
    )(given, near, bias)


def restore_kernel(back_ref, given_ref, out_ref):
    for core in range(2):
        out_ref[0, :, core * HD : (core + 1) * HD] = dot(back_ref[...], given_ref[core]).astype(BF16)


def restore(back, given):
    tok = back.shape[0]
    return pl.pallas_call(
        restore_kernel,
        out_shape=jax.ShapeDtypeStruct((1, tok, 2 * HD), BF16),
        in_specs=[VMEM, VMEM],
        out_specs=VMEM,
        compiler_params=pltpu.CompilerParams(vmem_limit_bytes=16 * MIB),
        name="restore",
    )(back, given)


def swap_all(value, axes):
    return lax.all_to_all(value, axes, split_axis=0, concat_axis=0, tiled=True)


def local(tokens, modality, doc_ids, owner_ids, norm_gain, query_weight, pair_weight):
    groups = lax.axis_size("grp")
    tok = tokens.shape[0]
    slots = tok // groups
    spread = pack(modality, owner_ids, doc_ids, query_weight, pair_weight, groups)
    weights = swap_all(spread, "grp")
    chosen = choose(modality, tokens)
    lifted = (chosen.astype(F32) * LIFT).astype(jnp.float16)
    gathered = lax.all_gather(lifted, "tp", axis=0)
    features = (gathered.astype(F32) * (1.0 / LIFT)).astype(BF16)
    keep, mine, give = project(normalize(features, norm_gain), weights)
    got = lax.ppermute(give, "tower", [(0, 1), (1, 0)])
    keep, later, owners = lax.optimization_barrier((keep, modality, owner_ids))
    sent = place(plan(later, owners, groups), keep, got, mine)
    sent, weights, later, owners = lax.optimization_barrier((sent, weights, later, owners))
    given = swap_all(sent.reshape(groups, slots, 2 * HD), "grp").reshape(tok, 2 * HD)
    bias, back = masks(weights, later, owners)
    near = lax.ppermute(given[:, HD:], "tp", [(t, t ^ 1) for t in range(lax.axis_size("tp"))])
    mixed = attend(given, near, bias)
    returned = swap_all(mixed.reshape(2 * groups, slots, HD), ("tower", "grp"))
    return restore(back, returned.reshape(2, tok, HD))


def solution(mesh):
    in_specs = (
        P("grp", "tp"),
        P("grp"),
        P("grp"),
        P("grp"),
        P("tower", None),
        P("tower", "grp", "tp"),
        P("tower", "grp", None),
    )
    out_specs = P("tower", "grp", "tp")
    return jax.shard_map(local, mesh=mesh, in_specs=in_specs, out_specs=out_specs, check_vma=False)
```

time: 183 us -> 159 us (0.87)
  waiting for transfers between devices: 22.6 us -> 2.27 us
  blocking collectives: 91.7 us -> 107 us
  local copies, waits for them, and re-layouts: 12.2 us -> 2.62 us
  starting transfers between devices: 26 us -> 21.5 us
  other arithmetic: 4.38 us -> 1.77 us
  Pallas kernels: 24.9 us -> 22.7 us
    all_to_all x2 -> x1, waiting for transfers between devices: 20.6 us -> 2.19 us  [swap_all(): return lax.all_to_all(value, axes, split_axis=0, concat_axis=0, tiled=True)]
    all_to_all x1 -> x2, blocking collectives: 13.9 us -> 29.5 us  [swap_all(): return lax.all_to_all(value, axes, split_axis=0, concat_axis=0, tiled=True)]
    all_to_all x2 -> x1, starting transfers between devices: 16 us -> 7.64 us  [swap_all(): return lax.all_to_all(value, axes, split_axis=0, concat_axis=0, tiled=True)]
    unnamed x16 -> x8, local copies, waits for them, and re-layouts: 10.1 us -> 2.61 us
    ppermute x1 -> x2, starting transfers between devices: 10 us -> 13.8 us  [the longest x1 7.2 us: local(): lax.ppermute(given[:, HD:], 'tp', [(t, t ^ 1) for t in range(lax.axis_siz...]
    convert_element_type x1, other arithmetic: 4.29 us -> 1.68 us  [local(): features = (gathered.astype(F32) * (1.0 / LIFT)).astype(BF16)]
    pallas_call x4 -> x7, Pallas kernels: 21.6 us -> 19.4 us  [the longest x1 5.48 us: project(): pl.pallas_call(project_kernel, out_shape=(jax.ShapeDtypeStruct((half, HD)...]
    broadcast_in_dim x3 -> x0, local copies, waits for them, and re-layouts: 2.07 us -> none  [the longest x1 0.69 us: prepare(): owner_ids[None]]
  transfers between devices with their start and end apart: 3 -> 3, of which waited for: 3 -> 2; matrix products, arithmetic and copies ran while one was open for 2% -> 1% of each run, Pallas kernels for 2% -> 6%
where the time goes in v2:
time: 159 us; the launch traced here: 158 us
  blocking collectives  107 us (67%)
  Pallas kernels  22.7 us (14%)
  starting transfers between devices  21.5 us (14%)
  local copies, waits for them, and re-layouts  2.62 us (2%)
  waiting for transfers between devices  2.27 us (1%)
  other arithmetic  1.77 us (1%)
    all_gather x1, blocking collectives, local(): gathered = lax.all_gather(lifted, 'tp', axis=0)  77.7 us
    all_to_all x2, blocking collectives, swap_all(): return lax.all_to_all(value, axes, split_axis=0, concat_axis=0, tiled=True)  29.5 us
    all_to_all x1, starting transfers between devices, swap_all(): return lax.all_to_all(value, axes, split_axis=0, concat_axis=0, tiled=True)  7.64 us
    ppermute x1, starting transfers between devices, local(): lax.ppermute(given[:, HD:], 'tp', [(t, t ^ 1) for t in range(lax.axis_siz...  7.2 us
    ppermute x1, starting transfers between devices, local(): got = lax.ppermute(give, 'tower', [(0, 1), (1, 0)])  6.63 us
    pallas_call x1, Pallas kernels, project(): pl.pallas_call(project_kernel, out_shape=(jax.ShapeDtypeStruct((half, HD)...  5.48 us
    pallas_call x1, Pallas kernels, pack(): pl.pallas_call(kernel, out_shape=pltpu.HBM((groups, rows + 16, cols), BF1...  3.99 us
    pallas_call x1, Pallas kernels, masks(): pl.pallas_call(mask_kernel, out_shape=(jax.ShapeDtypeStruct((tok, tok), B...  3.64 us
  transfers between devices with their start and end apart: 3, of which 2 were waited for; matrix products, arithmetic and copies ran while one was open for 1% of the time, Pallas kernels for 6%

profile of v2, /device:TPU:1, one launch (start us, length us, event | category | flops | bytes accessed | tf_op | source)
XLA Modules:
  0.0 158.2 jit_solution(10392541415619158993)
XLA Ops:
  0.0 4.0 %pack.1 = bf16[16,528,384]{2,1,0:T(8,128)(2,1)} custom-call(s32[768]{0:T(1024)} %modality_ref.5, s32[768]{0:T(1024)} %owner_ref.3, s32[768]{0:T(1024)} %doc_ref.1, bf16[1,512,256]{2,1,0:T(8,128)(2,1)} %query_ref.1, bf16[1,512,1024]{2,1,0:T(8,128)(2,1)} %pair_ref.1), custom_call_target="tpu_custom_call" | custom-call | tf_op jit(solution)/shard_map/pack/pallas_call | solution.py:144
  4.0 7.6 %all-to-all-start = ((bf16[16,528,384]{2,1,0:T(8,128)(2,1)}), bf16[16,528,384]{2,1,0:T(8,128)(2,1)}, u32[]{:S(2)}, u32[]{:S(2)}) async-start(bf16[16,528,384]{2,1,0:T(8,128)(2,1)} %pack.1), calls=%async_computation | async-start | bytes 12976128 | tf_op jit(solution)/shard_map/all_to_all | solution.py:447
  11.7 1.6 %choose.1 = bf16[384,512]{1,0:T(8,128)(2,1)S(1)} custom-call(s32[768]{0:T(1024)} %modality_ref.5, bf16[768,512]{1,0:T(8,128)(2,1)} %token_ref.1), custom_call_target="tpu_custom_call" | custom-call | tf_op jit(solution)/shard_map/choose/pallas_call | solution.py:181
  13.3 0.1 multiply_convert_fusion.1
  13.4 77.7 %all-gather.2 = f16[6144,512]{1,0:T(8,128)(2,1)S(1)} all-gather(f16[384,512]{1,0:T(8,128)(2,1)S(1)} %multiply_convert_fusion.1), channel_id=2, replica_groups=mesh['tower'=2,'tp'=16,'grp'=16] {'tp'}, dimensions={0}, use_global_device_ids=true | all-gather | bytes 6684672 | tf_op jit(solution)/shard_map/all_gather | solution.py:458
  91.1 1.7 %multiply_convert_fusion = bf16[6144,512]{1,0:T(8,128)(2,1)S(1)} fusion(f16[6144,512]{1,0:T(8,128)(2,1)S(1)} %all-gather.2), kind=kLoop, calls=%fused_computation | loop fusion | flops 9437184 | bytes 12582912 | tf_op jit(solution)/shard_map/convert_element_type | solution.py:459
  92.8 0.0 copy-done.3
  92.8 2.8 %normalize.1.normed_ref = bf16[16,384,512]{2,1,0:T(8,128)(2,1)S(1)} custom-call(bf16[16,384,512]{2,1,0:T(8,128)(2,1)S(1)} %bitcast.5, f32[1,8192]{1,0:T(1,128)S(1)} %copy-done.3), custom_call_target="tpu_custom_call" | custom-call | tf_op jit(solution)/shard_map/normalize/pallas_call | solution.py:217
  95.6 0.0 copy-start
  95.6 2.6 %copy-done = bf16[16,384,512]{2,1,0:T(8,128)(2,1)} copy-done((bf16[16,384,512]{2,1,0:T(8,128)(2,1)}, bf16[16,384,512]{2,1,0:T(8,128)(2,1)S(1)}, u32[]{:S(2)}) %copy-start) | copy-done | bytes 6291480
  98.2 2.2 %all-to-all-done.weight_ref.note_ref = bf16[16,528,384]{2,1,0:T(8,128)(2,1)} async-done(((bf16[16,528,384]{2,1,0:T(8,128)(2,1)}), bf16[16,528,384]{2,1,0:T(8,128)(2,1)}, u32[]{:S(2)}, u32[]{:S(2)}) %all-to-all-start) | async-done | bytes 6488096 | tf_op jit(solution)/shard_map/all_to_all | solution.py:447
  100.4 5.5 %project.1 = (bf16[384,128]{1,0:T(8,128)(2,1)S(1)}, bf16[384,128]{1,0:T(8,128)(2,1)S(1)}, bf16[384,256]{1,0:T(8,128)(2,1)S(1)}) custom-call(bf16[16,384,512]{2,1,0:T(8,128)(2,1)} %copy-done, bf16[16,528,384]{2,1,0:T(8,128)(2,1)} %all-to-all-done.weight_ref.note_ref), custom_call_target="tpu_custom_call" | custom-call | tf_op jit(solution)/shard_map/project/pallas_call | solution.py:271
  105.9 6.6 %collective-permute-start = (bf16[384,256]{1,0:T(8,128)(2,1)S(1)}, bf16[384,256]{1,0:T(8,128)(2,1)S(1)}, u32[]{:S(2)}, u32[]{:S(2)}) collective-permute-start(bf16[384,256]{1,0:T(8,128)(2,1)S(1)} %get-tuple-element.21), channel_id=1, source_target_pairs={{0,256},{256,0},{1,257},{257,1},{2,258},{258,2},{3,259},{259,3},{4... | collective-permute-start | bytes 589832 | tf_op jit(solution)/shard_map/ppermute | solution.py:461
  112.5 0.0 copy-done.1
  112.6 1.1 plan.1.place_ref
  113.6 0.0 collective-permute-done.got_ref
  113.6 0.8 place.1
  114.4 14.7 %all_to_all.15 = bf16[16,48,256]{2,1,0:T(8,128)(2,1)S(1)} all-to-all(bf16[16,48,256]{2,1,0:T(8,128)(2,1)S(1)} %bitcast.8), channel_id=1, replica_groups=mesh['tower'=2,'tp'=16,'grp'=16] {'grp'}, dimensions={0} | all-to-all | bytes 786432 | tf_op jit(solution)/shard_map/all_to_all | solution.py:447
  129.1 7.2 %collective-permute-start.1 = (bf16[768,128]{1,0:T(8,128)(2,1)S(1)}, bf16[768,128]{1,0:T(8,128)(2,1)S(1)}, u32[]{:S(2)}, u32[]{:S(2)}) collective-permute-start(bf16[768,128]{1,0:T(8,128)(2,1)S(1)} %slice.4), channel_id=1, source_target_pairs={{0,16},{16,0},{32,48},{48,32},{64,80},{80,64},{96,112},{112,96},{1... | collective-permute-start | bytes 589832 | tf_op jit(solution)/shard_map/ppermute | solution.py:467
  136.3 3.6 %masks.1 = (bf16[768,768]{1,0:T(8,128)(2,1)S(1)}, bf16[768,768]{1,0:T(8,128)(2,1)S(1)}) custom-call(bf16[16,528,384]{2,1,0:T(8,128)(2,1)} %all-to-all-done.weight_ref.note_ref, s32[768]{0:T(1024)S(1)} %copy-done.1, s32[768]{0:T(1024)S(1)} %copy-done.2), custom_call_target="tpu_custom_call" | custom-call | tf_op jit(solution)/shard_map/masks/pallas_call | solution.py:377
  139.9 0.1 collective-permute-done.1.near_ref
  140.0 1.8 %attend.1 = bf16[2,768,128]{2,1,0:T(8,128)(2,1)S(1)} custom-call(bf16[768,256]{1,0:T(8,128)(2,1)S(1)} %bitcast.7, bf16[768,128]{1,0:T(8,128)(2,1)S(1)} %collective-permute-done.1.near_ref, bf16[768,768]{1,0:T(8,128)(2,1)S(1)} %get-tuple-element.28.bias_ref), custom_call_target="tpu_custom_call" | custom-call | tf_op jit(solution)/shard_map/attend/pallas_call | solution.py:419
  141.8 14.8 %all_to_all.16 = bf16[32,48,128]{2,1,0:T(8,128)(2,1)S(1)} all-to-all(bf16[32,48,128]{2,1,0:T(8,128)(2,1)S(1)} %bitcast.9), channel_id=1, replica_groups=mesh['tower'=2,'tp'=16,'grp'=16] {'tower','grp'}, dimensions={0} | all-to-all | bytes 786432 | tf_op jit(solution)/shard_map/all_to_all | solution.py:447
  156.7 1.5 restore.1
  (5 shorter events, 0.0 us)
Async XLA Ops:
  4.0 96.4 %all-to-all-start = ((bf16[16,528,384]{2,1,0:T(8,128)(2,1)}), bf16[16,528,384]{2,1,0:T(8,128)(2,1)}, u32[]{:S(2)}, u32[]{:S(2)}) async-start(bf16[16,528,384]{2,1,0:T(8,128)(2,1)} %pack.1), calls=%async_computation | async-start | bytes 12976128 | tf_op jit(solution)/shard_map/all_to_all | solution.py:447
  91.1 1.7 %copy-start.3 = (f32[1,8192]{1,0:T(1,128)S(1)}, f32[1,8192]{1,0:T(1,128)}, u32[]{:S(2)}) copy-start(f32[1,8192]{1,0:T(1,128)} %gain_ref.1) | copy-start | bytes 98308
  95.6 2.6 %copy-start = (bf16[16,384,512]{2,1,0:T(8,128)(2,1)}, bf16[16,384,512]{2,1,0:T(8,128)(2,1)S(1)}, u32[]{:S(2)}) copy-start(bf16[16,384,512]{2,1,0:T(8,128)(2,1)S(1)} %normalize.1.normed_ref) | copy-start | bytes 18874372
  98.2 14.3 %copy-start.1 = (s32[768]{0:T(1024)S(1)}, s32[768]{0:T(1024)}, u32[]{:S(2)}) copy-start(s32[768]{0:T(1024)} %modality_ref.5) | copy-start | bytes 9220
  98.2 14.3 %copy-start.2 = (s32[768]{0:T(1024)S(1)}, s32[768]{0:T(1024)}, u32[]{:S(2)}) copy-start(s32[768]{0:T(1024)} %owner_ref.3) | copy-start | bytes 9220
  105.9 7.7 %collective-permute-start = (bf16[384,256]{1,0:T(8,128)(2,1)S(1)}, bf16[384,256]{1,0:T(8,128)(2,1)S(1)}, u32[]{:S(2)}, u32[]{:S(2)}) collective-permute-start(bf16[384,256]{1,0:T(8,128)(2,1)S(1)} %get-tuple-element.21), channel_id=1, source_target_pairs={{0,256},{256,0},{1,257},{257,1},{2,258},{258,2},{3,259},{259,3},{4... | collective-permute-start | bytes 589832 | tf_op jit(solution)/shard_map/ppermute | solution.py:461
  129.1 10.9 %collective-permute-start.1 = (bf16[768,128]{1,0:T(8,128)(2,1)S(1)}, bf16[768,128]{1,0:T(8,128)(2,1)S(1)}, u32[]{:S(2)}, u32[]{:S(2)}) collective-permute-start(bf16[768,128]{1,0:T(8,128)(2,1)S(1)} %slice.4), channel_id=1, source_target_pairs={{0,16},{16,0},{32,48},{48,32},{64,80},{80,64},{96,112},{112,96},{1... | collective-permute-start | bytes 589832 | tf_op jit(solution)/shard_map/ppermute | solution.py:467

commit v3 on v2

--- a/solution.py
+++ b/solution.py
@@ -77,45 +77,35 @@
 
 
 def pack_kernel(
-    groups, pair_heads, modality_ref, owner_ref, doc_ref, query_ref, pair_ref,
-    spread_ref, block, modality_own, owner_own, doc_own, sems,
+    groups, modality_ref, owner_ref, doc_ref, token_ref, query_ref, pair_ref,
+    chosen_ref, packed_ref, block, modality_own, owner_own, doc_own, token_own, sems,
 ):
-    tok = modality_ref.shape[0]
+    tok, half = token_ref.shape[0], chosen_ref.shape[0]
     rows, head_cols = query_ref.shape[1:]
-    cols = head_cols + HD
-    rank = lax.axis_index("tp")
-    per_head = lax.axis_size("tp") // pair_heads
-    column = (rank // per_head) * 2 * HD + (rank % 2) * HD
+    cols = packed_ref.shape[1]
+    pair_heads = pair_ref.shape[2] // (2 * HD)
+    column = lax.axis_index("tp") // (lax.axis_size("tp") // pair_heads) * 2 * HD
     sources = (
-        (query_ref.at[0], block.at[pl.ds(0, rows), pl.ds(0, head_cols)]),
-        (
-            pair_ref.at[0, :, pl.ds(pl.multiple_of(column, HD), HD)],
-            block.at[pl.ds(0, rows), pl.ds(head_cols, HD)],
-        ),
         (modality_ref, modality_own),
         (owner_ref, owner_own),
         (doc_ref, doc_own),
+        (query_ref.at[0], block.at[pl.ds(0, rows), pl.ds(0, head_cols)]),
+        (
+            pair_ref.at[0, :, pl.ds(pl.multiple_of(column, HD), 2 * HD)],
+            block.at[pl.ds(0, rows), pl.ds(head_cols, 2 * HD)],
+        ),
+        (token_ref, token_own),
     )
     loads = [
-        pltpu.make_async_copy(source, target, sems.at[2 * groups + k])
+        pltpu.make_async_copy(source, target, sems.at[k])
         for k, (source, target) in enumerate(sources)
     ]
     for copy in loads:
         copy.start()
-    for copy in loads[:2]:
-        copy.wait()
-    weights = [
-        pltpu.make_async_copy(
-            block.at[pl.ds(0, rows)], spread_ref.at[g, pl.ds(0, rows)], sems.at[g]
-        )
-        for g in range(groups)
-    ]
-    for copy in weights:
-        copy.start()
-    for copy in loads[2:]:
+    for copy in loads[:3]:
         copy.wait()
     modality = row_of(modality_own)
-    dest, _ = slots_of(modality, row_of(owner_own), groups)
+    dest, own_rank = slots_of(modality, row_of(owner_own), groups)
     high, low = split_number(iota((1, tok), 1))
     facts = stack_rows([row_of(doc_own).astype(F32), high, low, modality.astype(F32)])
     table = dot_nt(facts, ones_where(iota((tok, tok), 0) == dest))
@@ -124,73 +114,40 @@
     block[rows : rows + 16, :] = jnp.concatenate(
         [table[:, :cols], table[:, cols:]], axis=0
     ).astype(BF16)
-    notes = [
-        pltpu.make_async_copy(
-            block.at[pl.ds(rows, 16)], spread_ref.at[g, pl.ds(rows, 16)], sems.at[groups + g]
-        )
-        for g in range(groups)
-    ]
-    for copy in notes:
-        copy.start()
-    for copy in weights + notes:
+    for copy in loads[3:5]:
         copy.wait()
-
-
-def pack(modality, owner_ids, doc_ids, query_weight, pair_weight, groups):
-    tok = modality.shape[0]
+    store = pltpu.make_async_copy(block, packed_ref, sems.at[len(loads)])
+    store.start()
+    own_rank = jnp.where(modality == lax.axis_index("tower"), own_rank, half)
+    select = ones_where(iota((half, tok), 0) == own_rank)
+    loads[5].wait()
+    chosen_ref[...] = dot(select, token_own[...]).astype(BF16)
+    store.wait()
+
+
+def pack(modality, owner_ids, doc_ids, tokens, query_weight, pair_weight, groups):
+    tok, slab = tokens.shape
     rows, head_cols = query_weight.shape[1:]
-    cols = head_cols + HD
-    kernel = functools.partial(pack_kernel, groups, pair_weight.shape[2] // (2 * HD))
-    return pl.pallas_call(
-        kernel,
-        out_shape=pltpu.HBM((groups, rows + 16, cols), BF16),
-        in_specs=[HBM] * 5,
-        out_specs=HBM,
+    cols = head_cols + 2 * HD
+    return pl.pallas_call(
+        functools.partial(pack_kernel, groups),
+        out_shape=(
+            jax.ShapeDtypeStruct((tok // 2, slab), BF16),
+            pltpu.HBM((rows + 16, cols), BF16),
+        ),
+        in_specs=[HBM] * 6,
+        out_specs=(VMEM, HBM),
         scratch_shapes=[
             pltpu.VMEM((rows + 16, cols), BF16),
             pltpu.VMEM((tok,), I32),
             pltpu.VMEM((tok,), I32),
             pltpu.VMEM((tok,), I32),
-            pltpu.SemaphoreType.DMA((2 * groups + 5,)),
+            pltpu.VMEM((tok, slab), BF16),
+            pltpu.SemaphoreType.DMA((7,)),
         ],
-        compiler_params=pltpu.CompilerParams(vmem_limit_bytes=16 * MIB),
+        compiler_params=pltpu.CompilerParams(vmem_limit_bytes=24 * MIB),
         name="pack",
-    )(*in_hbm(modality, owner_ids, doc_ids, query_weight, pair_weight))
-
-
-def choose_kernel(modality_ref, token_ref, chosen_ref, modality_own, token_own, sems):
-    tok, half = token_ref.shape[0], chosen_ref.shape[0]
-    loads = (
-        pltpu.make_async_copy(modality_ref, modality_own, sems.at[0]),
-        pltpu.make_async_copy(token_ref, token_own, sems.at[1]),
-    )
-    for copy in loads:
-        copy.start()
-    loads[0].wait()
-    mine = row_of(modality_own) == lax.axis_index("tower")
-    before = ones_where(iota((tok, tok), 0) < iota((tok, tok), 1))
-    flags = jnp.broadcast_to(jnp.where(mine, 1.0, 0.0), (8, tok)).astype(BF16)
-    rank = jnp.where(mine, dot(flags, before)[0:1].astype(I32), half)
-    select = ones_where(iota((half, tok), 0) == rank)
-    loads[1].wait()
-    chosen_ref[...] = dot(select, token_own[...]).astype(BF16)
-
-
-def choose(modality, tokens):
-    tok, slab = tokens.shape
-    return pl.pallas_call(
-        choose_kernel,
-        out_shape=jax.ShapeDtypeStruct((tok // 2, slab), BF16),
-        in_specs=[HBM, HBM],
-        out_specs=VMEM,
-        scratch_shapes=[
-            pltpu.VMEM((tok,), I32),
-            pltpu.VMEM((tok, slab), BF16),
-            pltpu.SemaphoreType.DMA((2,)),
-        ],
-        compiler_params=pltpu.CompilerParams(vmem_limit_bytes=16 * MIB),
-        name="choose",
-    )(*in_hbm(modality, tokens))
+    )(*in_hbm(modality, owner_ids, doc_ids, tokens, query_weight, pair_weight))
 
 
 def normalize_kernel(feature_ref, gain_ref, out_ref):
@@ -248,9 +205,9 @@
         term = fold([dot(rows[k], block[k]) for k in range(at, at + together)])
         total = term if total is None else total + term
     total = total.astype(BF16)
-    mine = total[:, 2 * HD :]
-    mine_ref[...] = mine
-    give_ref[:, HD:] = mine
+    pair = total[:, 2 * HD :]
+    mine_ref[...] = pair
+    give_ref[:, HD:] = pair
     text = lax.axis_index("tower") == 0
 
     @pl.when(text)
@@ -267,13 +224,13 @@
 def project(normed, weights):
     count, half, slab = normed.shape
     groups, rows, cols = weights.shape
-    assert groups == count and rows == slab + 16 and cols == 3 * HD
+    assert groups == count and rows == slab + 16 and cols == 4 * HD
     return pl.pallas_call(
         project_kernel,
         out_shape=(
             jax.ShapeDtypeStruct((half, HD), BF16),
-            jax.ShapeDtypeStruct((half, HD), BF16),
             jax.ShapeDtypeStruct((half, 2 * HD), BF16),
+            jax.ShapeDtypeStruct((half, 3 * HD), BF16),
         ),
         in_specs=[HBM, HBM],
         out_specs=(VMEM,) * 3,
@@ -323,7 +280,7 @@
     tok = where.shape[0]
     return pl.pallas_call(
         place_kernel,
-        out_shape=jax.ShapeDtypeStruct((tok, 2 * HD), BF16),
+        out_shape=jax.ShapeDtypeStruct((tok, 3 * HD), BF16),
         in_specs=[VMEM] * 4,
         out_specs=VMEM,
         compiler_params=pltpu.CompilerParams(vmem_limit_bytes=16 * MIB),
@@ -388,42 +345,30 @@
     )(*in_hbm(weights), modality, owner_ids)
 
 
-def attend_kernel(given_ref, near_ref, bias_ref, out_ref):
+def attend_kernel(given_ref, bias_ref, out_ref):
     tok = given_ref.shape[0]
-    mine = given_ref[:, HD:]
+    keys, values = given_ref[:, HD : 2 * HD], given_ref[:, 2 * HD :]
     tile = min(256, tok)
-
-    def run(keys, values):
-        for at in range(0, tok, tile):
-            scores = dot_nt(given_ref[at : at + tile, :HD], keys) * (1.0 / math.sqrt(HD))
-            scores = scores + bias_ref[at : at + tile, :].astype(F32)
-            powered = jnp.exp(scores - jnp.max(scores, axis=1, keepdims=True))
-            inverse = 1.0 / jnp.sum(powered, axis=1, keepdims=True)
-            mixed = dot((powered * inverse).astype(BF16), values).astype(BF16)
-            out_ref[0, at : at + tile, :] = mixed
-            out_ref[1, at : at + tile, :] = mixed
-
-    even = lax.axis_index("tp") % 2 == 0
-
-    @pl.when(even)
-    def _():
-        run(mine, near_ref[...])
-
-    @pl.when(jnp.logical_not(even))
-    def _():
-        run(near_ref[...], mine)
-
-
-def attend(given, near, bias):
+    for at in range(0, tok, tile):
+        scores = dot_nt(given_ref[at : at + tile, :HD], keys) * (1.0 / math.sqrt(HD))
+        scores = scores + bias_ref[at : at + tile, :].astype(F32)
+        powered = jnp.exp(scores - jnp.max(scores, axis=1, keepdims=True))
+        inverse = 1.0 / jnp.sum(powered, axis=1, keepdims=True)
+        mixed = dot((powered * inverse).astype(BF16), values).astype(BF16)
+        out_ref[0, at : at + tile, :] = mixed
+        out_ref[1, at : at + tile, :] = mixed
+
+
+def attend(given, bias):
     tok = bias.shape[0]
     return pl.pallas_call(
         attend_kernel,
         out_shape=jax.ShapeDtypeStruct((2, tok, HD), BF16),
-        in_specs=[VMEM] * 3,
+        in_specs=[VMEM, VMEM],
         out_specs=VMEM,
         compiler_params=pltpu.CompilerParams(vmem_limit_bytes=24 * MIB),
         name="attend",
-    )(given, near, bias)
+    )(given, bias)
 
 
 def restore_kernel(back_ref, given_ref, out_ref):
@@ -451,21 +396,24 @@
     groups = lax.axis_size("grp")
     tok = tokens.shape[0]
     slots = tok // groups
-    spread = pack(modality, owner_ids, doc_ids, query_weight, pair_weight, groups)
-    weights = swap_all(spread, "grp")
-    chosen = choose(modality, tokens)
+    chosen, packed = pack(
+        modality, owner_ids, doc_ids, tokens, query_weight, pair_weight, groups
+    )
+    weights = lax.all_gather(packed, "grp", axis=0)
     lifted = (chosen.astype(F32) * LIFT).astype(jnp.float16)
     gathered = lax.all_gather(lifted, "tp", axis=0)
     features = (gathered.astype(F32) * (1.0 / LIFT)).astype(BF16)
-    keep, mine, give = project(normalize(features, norm_gain), weights)
+    normed, later, owners = lax.optimization_barrier(
+        (normalize(features, norm_gain), modality, owner_ids)
+    )
+    where = plan(later, owners, groups)
+    keep, mine, give = project(normed, weights)
     got = lax.ppermute(give, "tower", [(0, 1), (1, 0)])
-    keep, later, owners = lax.optimization_barrier((keep, modality, owner_ids))
-    sent = place(plan(later, owners, groups), keep, got, mine)
+    sent = place(where, keep, got, mine)
     sent, weights, later, owners = lax.optimization_barrier((sent, weights, later, owners))
-    given = swap_all(sent.reshape(groups, slots, 2 * HD), "grp").reshape(tok, 2 * HD)
+    given = swap_all(sent.reshape(groups, slots, 3 * HD), "grp").reshape(tok, 3 * HD)
     bias, back = masks(weights, later, owners)
-    near = lax.ppermute(given[:, HD:], "tp", [(t, t ^ 1) for t in range(lax.axis_size("tp"))])
-    mixed = attend(given, near, bias)
+    mixed = attend(given, bias)
     returned = swap_all(mixed.reshape(2 * groups, slots, HD), ("tower", "grp"))
     return restore(back, returned.reshape(2, tok, HD))
 

time: 159 us -> 156 us (0.981)
  starting transfers between devices: 21.5 us -> 7.55 us
  blocking collectives: 107 us -> 93.5 us
  between operations: 0.14 us -> 13.5 us
  waiting for transfers between devices: 2.27 us -> 15.2 us
  Pallas kernels: 22.7 us -> 21.1 us
    all_to_all x2 -> x1, blocking collectives: 29.5 us -> 14.2 us  [swap_all(): return lax.all_to_all(value, axes, split_axis=0, concat_axis=0, tiled=True)]
    all_gather x0 -> x1, waiting for transfers between devices: none -> 7.37 us  [local(): weights = lax.all_gather(packed, 'grp', axis=0)]
    ppermute x1 -> x0, starting transfers between devices: 7.2 us -> none  [local(): lax.ppermute(given[:, HD:], 'tp', [(t, t ^ 1) for t in range(lax.axis_siz...]
    all_to_all x1, waiting for transfers between devices: 2.19 us -> 7.75 us  [swap_all(): return lax.all_to_all(value, axes, split_axis=0, concat_axis=0, tiled=True)]
    ppermute x1, starting transfers between devices: 6.63 us -> 2.58 us  [local(): got = lax.ppermute(give, 'tower', [(0, 1), (1, 0)])]
    all_to_all x1, starting transfers between devices: 7.64 us -> 4.97 us  [swap_all(): return lax.all_to_all(value, axes, split_axis=0, concat_axis=0, tiled=True)]
    pallas_call x3 -> x2, Pallas kernels: 6.41 us -> 4.19 us  [the longest x1 2.41 us: pack(): pl.pallas_call(functools.partial(pack_kernel, groups), out_shape=(jax.Sha...]
  transfers between devices with their start and end apart: 3 -> 3, of which waited for: 2 -> 3; matrix products, arithmetic and copies ran while one was open for 1% -> 1% of each run, Pallas kernels for 6% -> 5%
where the time goes in v3:
time: 156 us; the launch traced here: 155 us
  blocking collectives  93.5 us (60%)
  Pallas kernels  21.1 us (14%)
  waiting for transfers between devices  15.2 us (10%)
  between operations  13.5 us (9%)
  starting transfers between devices  7.55 us (5%)
  local copies, waits for them, and re-layouts  2.7 us (2%)
  other arithmetic  1.77 us (1%)
    all_gather x1, blocking collectives, local(): gathered = lax.all_gather(lifted, 'tp', axis=0)  79.3 us
    all_to_all x1, blocking collectives, swap_all(): return lax.all_to_all(value, axes, split_axis=0, concat_axis=0, tiled=True)  14.2 us
    all_to_all x1, waiting for transfers between devices, swap_all(): return lax.all_to_all(value, axes, split_axis=0, concat_axis=0, tiled=True)  7.75 us
    all_gather x1, waiting for transfers between devices, local(): weights = lax.all_gather(packed, 'grp', axis=0)  7.37 us
    pallas_call x1, Pallas kernels, project(): pl.pallas_call(project_kernel, out_shape=(jax.ShapeDtypeStruct((half, HD)...  6.06 us
    all_to_all x1, starting transfers between devices, swap_all(): return lax.all_to_all(value, axes, split_axis=0, concat_axis=0, tiled=True)  4.97 us
    pallas_call x1, Pallas kernels, masks(): pl.pallas_call(mask_kernel, out_shape=(jax.ShapeDtypeStruct((tok, tok), B...  3.66 us
  transfers between devices with their start and end apart: 3, of which 3 were waited for; matrix products, arithmetic and copies ran while one was open for 1% of the time, Pallas kernels for 5%

profile of v3, /device:TPU:1, one launch (start us, length us, event | category | flops | bytes accessed | tf_op | source)
XLA Modules:
  0.0 155.4 jit_solution(2437240098114097777)
XLA Ops:
  6.5 0.0 all-gather.5.cloned.1.call-start
  6.5 2.4 %pack.1 = (bf16[384,512]{1,0:T(8,128)(2,1)S(1)}, bf16[528,512]{1,0:T(8,128)(2,1)}) custom-call(s32[768]{0:T(1024)} %modality_ref.3, s32[768]{0:T(1024)} %owner_ref.3, s32[768]{0:T(1024)} %doc_ref.1, bf16[768,512]{1,0:T(8,128)(2,1)} %token_ref.1, bf16[1,512,256]{2,1,0:T(8,128)(2,1)} %query_ref.1, bf16[1,512,1024]{2,1,0:T(8,128)(2,1)} %pair_ref.1), custom_call_target="tpu_custom_call" | custom-call | tf_op jit(solution)/shard_map/pack/pallas_call | solution.py:132
  9.0 0.0 all-gather.5.cloned.1.call-update
  9.0 0.1 multiply_convert_fusion.1
  9.1 79.3 %all-gather.6 = f16[6144,512]{1,0:T(8,128)(2,1)S(1)} all-gather(f16[384,512]{1,0:T(8,128)(2,1)S(1)} %multiply_convert_fusion.1), channel_id=2, replica_groups=mesh['tower'=2,'tp'=16,'grp'=16] {'tp'}, dimensions={0}, use_global_device_ids=true | all-gather | bytes 6684672 | tf_op jit(solution)/shard_map/all_gather | solution.py:404
  88.4 1.7 %multiply_convert_fusion = bf16[6144,512]{1,0:T(8,128)(2,1)S(1)} fusion(f16[6144,512]{1,0:T(8,128)(2,1)S(1)} %all-gather.6), kind=kLoop, calls=%fused_computation | loop fusion | flops 9437184 | bytes 12582912 | tf_op jit(solution)/shard_map/convert_element_type | solution.py:405
  90.1 0.0 copy-done.3
  90.1 2.8 %normalize.1.normed_ref = bf16[16,384,512]{2,1,0:T(8,128)(2,1)S(1)} custom-call(bf16[16,384,512]{2,1,0:T(8,128)(2,1)S(1)} %bitcast.6, f32[1,8192]{1,0:T(1,128)S(1)} %copy-done.3), custom_call_target="tpu_custom_call" | custom-call | tf_op jit(solution)/shard_map/normalize/pallas_call | solution.py:174
  92.9 0.0 copy-start
  92.9 2.7 %copy-done = bf16[16,384,512]{2,1,0:T(8,128)(2,1)} copy-done((bf16[16,384,512]{2,1,0:T(8,128)(2,1)}, bf16[16,384,512]{2,1,0:T(8,128)(2,1)S(1)}, u32[]{:S(2)}) %copy-start) | copy-done | bytes 6291480
  95.6 7.4 %all-gather.5.cloned.1.call-done = bf16[8448,512]{1,0:T(8,128)(2,1)} async-done(((bf16[528,512]{1,0:T(8,128)(2,1)}), bf16[8448,512]{1,0:T(8,128)(2,1)}) %all-gather.5.cloned.1.call-update) | async-done | bytes 8650768 | tf_op jit(solution)/shard_map/all_gather | solution.py:402
  103.0 6.1 %project.1 = (bf16[384,128]{1,0:T(8,128)(2,1)S(1)}, bf16[384,256]{1,0:T(8,128)(2,1)S(1)}, bf16[384,384]{1,0:T(8,128)(2,1)S(1)}) custom-call(bf16[16,384,512]{2,1,0:T(8,128)(2,1)} %copy-done, bf16[16,528,512]{2,1,0:T(8,128)(2,1)} %bitcast.10), custom_call_target="tpu_custom_call" | custom-call | tf_op jit(solution)/shard_map/project/pallas_call | solution.py:228
  109.0 2.6 %collective-permute-start = (bf16[384,384]{1,0:T(8,128)(2,1)S(1)}, bf16[384,384]{1,0:T(8,128)(2,1)S(1)}, u32[]{:S(2)}, u32[]{:S(2)}) collective-permute-start(bf16[384,384]{1,0:T(8,128)(2,1)S(1)} %get-tuple-element.25), channel_id=1, source_target_pairs={{0,256},{256,0},{1,257},{257,1},{2,258},{258,2},{3,259},{259,3},{4... | collective-permute-start | bytes 884744 | tf_op jit(solution)/shard_map/ppermute | solution.py:411
  111.6 0.0 copy-done.1
  111.6 0.0 copy-done.2
  111.6 1.1 plan.1.place_ref
  112.7 0.1 collective-permute-done.got_ref
  112.8 1.8 %place.1 = bf16[768,384]{1,0:T(8,128)(2,1)} custom-call(bf16[768,768]{1,0:T(8,128)(2,1)S(1)} %plan.1.place_ref, bf16[384,128]{1,0:T(8,128)(2,1)S(1)} %get-tuple-element.24.keep_ref, bf16[384,384]{1,0:T(8,128)(2,1)S(1)} %collective-permute-done.got_ref, bf16[384,256]{1,0:T(8,128)(2,1)S(1)} %get-tuple-element.26.mine_ref), custom_call_target="tpu_custom_call" | custom-call | tf_op jit(solution)/shard_map/place/pallas_call | solution.py:281
  114.6 5.0 %all-to-all-start = ((bf16[16,48,384]{2,1,0:T(8,128)(2,1)}), bf16[16,48,384]{2,1,0:T(8,128)(2,1)S(1)}, u32[]{:S(2)}, u32[]{:S(2)}) async-start(bf16[16,48,384]{2,1,0:T(8,128)(2,1)} %bitcast.2), calls=%async_computation | async-start | bytes 1179648 | tf_op jit(solution)/shard_map/all_to_all | solution.py:392
  119.6 3.7 %masks.1 = (bf16[768,768]{1,0:T(8,128)(2,1)S(1)}, bf16[768,768]{1,0:T(8,128)(2,1)S(1)}) custom-call(bf16[16,528,512]{2,1,0:T(8,128)(2,1)} %bitcast.11, s32[768]{0:T(1024)S(1)} %copy-done.1, s32[768]{0:T(1024)S(1)} %copy-done.2), custom_call_target="tpu_custom_call" | custom-call | tf_op jit(solution)/shard_map/masks/pallas_call | solution.py:334
  123.2 7.7 %all-to-all-done = bf16[16,48,384]{2,1,0:T(8,128)(2,1)S(1)} async-done(((bf16[16,48,384]{2,1,0:T(8,128)(2,1)}), bf16[16,48,384]{2,1,0:T(8,128)(2,1)S(1)}, u32[]{:S(2)}, u32[]{:S(2)}) %all-to-all-start) | async-done | bytes 589856 | tf_op jit(solution)/shard_map/all_to_all | solution.py:392
  131.0 1.8 %attend.1 = bf16[2,768,128]{2,1,0:T(8,128)(2,1)S(1)} custom-call(bf16[768,384]{1,0:T(8,128)(2,1)S(1)} %bitcast.7, bf16[768,768]{1,0:T(8,128)(2,1)S(1)} %get-tuple-element.32.bias_ref), custom_call_target="tpu_custom_call" | custom-call | tf_op jit(solution)/shard_map/attend/pallas_call | solution.py:364
  132.8 14.2 %all_to_all.10 = bf16[32,48,128]{2,1,0:T(8,128)(2,1)S(1)} all-to-all(bf16[32,48,128]{2,1,0:T(8,128)(2,1)S(1)} %bitcast.9), channel_id=1, replica_groups=mesh['tower'=2,'tp'=16,'grp'=16] {'tower','grp'}, dimensions={0} | all-to-all | bytes 786432 | tf_op jit(solution)/shard_map/all_to_all | solution.py:392
  147.0 1.5 restore.1
  (3 shorter events, 0.0 us)
Async XLA Ops:
  6.5 96.4 %all-gather.5.cloned.1.call-start = ((), (), s32[]{:S(2)}) async-start(), calls=%async_computation.2 | async-start | bytes 9191424 | tf_op jit(solution)/shard_map/all_gather | solution.py:402
  88.4 1.7 %copy-start.3 = (f32[1,8192]{1,0:T(1,128)S(1)}, f32[1,8192]{1,0:T(1,128)}, u32[]{:S(2)}) copy-start(f32[1,8192]{1,0:T(1,128)} %gain_ref.1) | copy-start | bytes 98308
  92.9 2.7 %copy-start = (bf16[16,384,512]{2,1,0:T(8,128)(2,1)}, bf16[16,384,512]{2,1,0:T(8,128)(2,1)S(1)}, u32[]{:S(2)}) copy-start(bf16[16,384,512]{2,1,0:T(8,128)(2,1)S(1)} %normalize.1.normed_ref) | copy-start | bytes 18874372
  103.0 8.7 %copy-start.1 = (s32[768]{0:T(1024)S(1)}, s32[768]{0:T(1024)}, u32[]{:S(2)}) copy-start(s32[768]{0:T(1024)} %modality_ref.3) | copy-start | bytes 9220
  103.0 8.7 %copy-start.2 = (s32[768]{0:T(1024)S(1)}, s32[768]{0:T(1024)}, u32[]{:S(2)}) copy-start(s32[768]{0:T(1024)} %owner_ref.3) | copy-start | bytes 9220
  109.0 3.8 %collective-permute-start = (bf16[384,384]{1,0:T(8,128)(2,1)S(1)}, bf16[384,384]{1,0:T(8,128)(2,1)S(1)}, u32[]{:S(2)}, u32[]{:S(2)}) collective-permute-start(bf16[384,384]{1,0:T(8,128)(2,1)S(1)} %get-tuple-element.25), channel_id=1, source_target_pairs={{0,256},{256,0},{1,257},{257,1},{2,258},{258,2},{3,259},{259,3},{4... | collective-permute-start | bytes 884744 | tf_op jit(solution)/shard_map/ppermute | solution.py:411
  114.6 16.4 %all-to-all-start = ((bf16[16,48,384]{2,1,0:T(8,128)(2,1)}), bf16[16,48,384]{2,1,0:T(8,128)(2,1)S(1)}, u32[]{:S(2)}, u32[]{:S(2)}) async-start(bf16[16,48,384]{2,1,0:T(8,128)(2,1)} %bitcast.2), calls=%async_computation | async-start | bytes 1179648 | tf_op jit(solution)/shard_map/all_to_all | solution.py:392
Sparse Core Ops, SparseCore 0:
  10.4 92.5 all-gather.4

commit v4 on v3

--- a/solution.py
+++ b/solution.py
@@ -150,8 +150,9 @@
     )(*in_hbm(modality, owner_ids, doc_ids, tokens, query_weight, pair_weight))
 
 
-def normalize_kernel(feature_ref, gain_ref, out_ref):
+def normalize_kernel(feature_ref, gain_ref, early_ref, late_ref):
     count, half, slab = feature_ref.shape
+    early = early_ref.shape[0]
     tile = 48 if half % 48 == 0 else 16
 
     @pl.loop(0, half // tile)
@@ -167,42 +168,56 @@
         for k in range(count):
             values = feature_ref[k, at, :].astype(F32) * inverse
             gain = gain_ref[:, k * slab : (k + 1) * slab]
-            out_ref[k, at, :] = (values * gain).astype(BF16)
+            normed = (values * gain).astype(BF16)
+            if k < early:
+                early_ref[k, at, :] = normed
+            else:
+                late_ref[k - early, at, :] = normed
 
 
 def normalize(features, gain):
+    count, half, slab = features.shape
+    early = count // 2
     return pl.pallas_call(
         normalize_kernel,
-        out_shape=jax.ShapeDtypeStruct(features.shape, BF16),
+        out_shape=(
+            jax.ShapeDtypeStruct((early, half, slab), BF16),
+            jax.ShapeDtypeStruct((count - early, half, slab), BF16),
+        ),
         in_specs=[VMEM, VMEM],
-        out_specs=VMEM,
+        out_specs=(VMEM, VMEM),
         compiler_params=pltpu.CompilerParams(vmem_limit_bytes=20 * MIB),
         name="normalize",
     )(features, gain)
 
 
-def project_kernel(normed_ref, weight_ref, keep_ref, mine_ref, give_ref, rows, block, sems):
-    count, _, slab = normed_ref.shape
-    loads = []
+def project_kernel(
+    early_ref, late_ref, weight_ref, keep_ref, mine_ref, give_ref, rows, block, sems
+):
+    early, _, slab = early_ref.shape
+    count = early + late_ref.shape[0]
+    weights = [
+        pltpu.make_async_copy(weight_ref.at[k, pl.ds(0, slab)], block.at[k], sems.at[k])
+        for k in range(count)
+    ]
+    lates = [
+        pltpu.make_async_copy(late_ref.at[k], rows.at[k], sems.at[count + k])
+        for k in range(count - early)
+    ]
     for k in range(count):
-        loads.append(
-            (
-                pltpu.make_async_copy(normed_ref.at[k], rows.at[k], sems.at[2 * k]),
-                pltpu.make_async_copy(
-                    weight_ref.at[k, pl.ds(0, slab)], block.at[k], sems.at[2 * k + 1]
-                ),
-            )
-        )
-    for pair in loads:
-        for copy in pair:
-            copy.start()
+        weights[k].start()
+        if k >= early:
+            lates[k - early].start()
     total = None
-    together = 2
+    together = 1
     for at in range(0, count, together):
-        for pair in loads[at : at + together]:
-            for copy in pair:
-                copy.wait()
-        term = fold([dot(rows[k], block[k]) for k in range(at, at + together)])
+        terms = []
+        for k in range(at, at + together):
+            weights[k].wait()
+            if k >= early:
+                lates[k - early].wait()
+            terms.append(dot(early_ref[k] if k < early else rows[k - early], block[k]))
+        term = fold(terms)
         total = term if total is None else total + term
     total = total.astype(BF16)
     pair = total[:, 2 * HD :]
@@ -222,9 +237,10 @@
 
 
 def project(normed, weights):
-    count, half, slab = normed.shape
+    early, late = normed
+    _, half, slab = early.shape
     groups, rows, cols = weights.shape
-    assert groups == count and rows == slab + 16 and cols == 4 * HD
+    assert groups == len(early) + len(late) and rows == slab + 16 and cols == 4 * HD
     return pl.pallas_call(
         project_kernel,
         out_shape=(
@@ -232,16 +248,16 @@
             jax.ShapeDtypeStruct((half, 2 * HD), BF16),
             jax.ShapeDtypeStruct((half, 3 * HD), BF16),
         ),
-        in_specs=[HBM, HBM],
+        in_specs=[VMEM, HBM, HBM],
         out_specs=(VMEM,) * 3,
         scratch_shapes=[
-            pltpu.VMEM((count, half, slab), BF16),
-            pltpu.VMEM((count, slab, cols), BF16),
-            pltpu.SemaphoreType.DMA((2 * count,)),
+            pltpu.VMEM(late.shape, BF16),
+            pltpu.VMEM((groups, slab, cols), BF16),
+            pltpu.SemaphoreType.DMA((groups + len(late),)),
         ],
-        compiler_params=pltpu.CompilerParams(vmem_limit_bytes=32 * MIB),
+        compiler_params=pltpu.CompilerParams(vmem_limit_bytes=24 * MIB),
         name="project",
-    )(*in_hbm(normed, weights))
+    )(early, *in_hbm(late, weights))
 
 
 def plan_kernel(groups, modality_ref, owner_ref, place_ref):
@@ -270,10 +286,9 @@
 
 
 def place_kernel(place_ref, keep_ref, got_ref, mine_ref, out_ref):
-    half = keep_ref.shape[0]
-    own, other = place_ref[:, :half], place_ref[:, half:]
-    out_ref[:, :HD] = (dot(own, keep_ref[...]) + dot(other, got_ref[:, :HD])).astype(BF16)
-    out_ref[:, HD:] = (dot(own, mine_ref[...]) + dot(other, got_ref[:, HD:])).astype(BF16)
+    own = jnp.concatenate([keep_ref[...], mine_ref[...]], axis=1)
+    rows = jnp.concatenate([own, got_ref[...]], axis=0)
+    out_ref[...] = dot(place_ref[...], rows).astype(BF16)
 
 
 def place(where, keep, got, mine):
@@ -372,8 +387,8 @@
 
 
 def restore_kernel(back_ref, given_ref, out_ref):
-    for core in range(2):
-        out_ref[0, :, core * HD : (core + 1) * HD] = dot(back_ref[...], given_ref[core]).astype(BF16)
+    both = jnp.concatenate([given_ref[0], given_ref[1]], axis=1)
+    out_ref[0] = dot(back_ref[...], both).astype(BF16)
 
 
 def restore(back, given):
@@ -403,13 +418,10 @@
     lifted = (chosen.astype(F32) * LIFT).astype(jnp.float16)
     gathered = lax.all_gather(lifted, "tp", axis=0)
     features = (gathered.astype(F32) * (1.0 / LIFT)).astype(BF16)
-    normed, later, owners = lax.optimization_barrier(
-        (normalize(features, norm_gain), modality, owner_ids)
-    )
-    where = plan(later, owners, groups)
-    keep, mine, give = project(normed, weights)
+    keep, mine, give = project(normalize(features, norm_gain), weights)
     got = lax.ppermute(give, "tower", [(0, 1), (1, 0)])
-    sent = place(where, keep, got, mine)
+    keep, later, owners = lax.optimization_barrier((keep, modality, owner_ids))
+    sent = place(plan(later, owners, groups), keep, got, mine)
     sent, weights, later, owners = lax.optimization_barrier((sent, weights, later, owners))
     given = swap_all(sent.reshape(groups, slots, 3 * HD), "grp").reshape(tok, 3 * HD)
     bias, back = masks(weights, later, owners)

time: 156 us -> 155 us (level)
  no operation moved by 1% of the time
where the time goes in v4:
time: 155 us
  blocking collectives  93.5 us (60%)
  Pallas kernels  20.2 us (13%)
  waiting for transfers between devices  16.3 us (11%)
  between operations  13.5 us (9%)
  starting transfers between devices  7.56 us (5%)
  other arithmetic  1.77 us (1%)
  local copies, waits for them, and re-layouts  1.67 us (1%)
    all_gather x1, blocking collectives, local(): gathered = lax.all_gather(lifted, 'tp', axis=0)  79.3 us
    all_to_all x1, blocking collectives, swap_all(): return lax.all_to_all(value, axes, split_axis=0, concat_axis=0, tiled=True)  14.2 us
    all_gather x1, waiting for transfers between devices, local(): weights = lax.all_gather(packed, 'grp', axis=0)  8.4 us
    all_to_all x1, waiting for transfers between devices, swap_all(): return lax.all_to_all(value, axes, split_axis=0, concat_axis=0, tiled=True)  7.74 us
    pallas_call x1, Pallas kernels, project(): pl.pallas_call(project_kernel, out_shape=(jax.ShapeDtypeStruct((half, HD)...  5.6 us
    all_to_all x1, starting transfers between devices, swap_all(): return lax.all_to_all(value, axes, split_axis=0, concat_axis=0, tiled=True)  4.98 us
    pallas_call x1, Pallas kernels, masks(): pl.pallas_call(mask_kernel, out_shape=(jax.ShapeDtypeStruct((tok, tok), B...  3.66 us
  transfers between devices with their start and end apart: 3, of which 3 were waited for; matrix products, arithmetic and copies ran while one was open for 1% of the time, Pallas kernels for 5%

profile of v4, /device:TPU:1, one launch (start us, length us, event | category | flops | bytes accessed | tf_op | source)
XLA Modules:
  0.0 154.5 jit_solution(2930145155214021501)
XLA Ops:
  6.5 0.0 all-gather.5.cloned.1.call-start
  6.5 2.4 %pack.1 = (bf16[384,512]{1,0:T(8,128)(2,1)S(1)}, bf16[528,512]{1,0:T(8,128)(2,1)}) custom-call(s32[768]{0:T(1024)} %modality_ref.3, s32[768]{0:T(1024)} %owner_ref.3, s32[768]{0:T(1024)} %doc_ref.1, bf16[768,512]{1,0:T(8,128)(2,1)} %token_ref.1, bf16[1,512,256]{2,1,0:T(8,128)(2,1)} %query_ref.1, bf16[1,512,1024]{2,1,0:T(8,128)(2,1)} %pair_ref.1), custom_call_target="tpu_custom_call" | custom-call | tf_op jit(solution)/shard_map/pack/pallas_call | solution.py:132
  9.0 0.0 all-gather.5.cloned.1.call-update
  9.0 0.1 multiply_convert_fusion.1
  9.1 79.3 %all-gather.6 = f16[6144,512]{1,0:T(8,128)(2,1)S(1)} all-gather(f16[384,512]{1,0:T(8,128)(2,1)S(1)} %multiply_convert_fusion.1), channel_id=2, replica_groups=mesh['tower'=2,'tp'=16,'grp'=16] {'tp'}, dimensions={0}, use_global_device_ids=true | all-gather | bytes 6684672 | tf_op jit(solution)/shard_map/all_gather | solution.py:419
  88.4 1.7 %multiply_convert_fusion = bf16[6144,512]{1,0:T(8,128)(2,1)S(1)} fusion(f16[6144,512]{1,0:T(8,128)(2,1)S(1)} %all-gather.6), kind=kLoop, calls=%fused_computation | loop fusion | flops 9437184 | bytes 12582912 | tf_op jit(solution)/shard_map/convert_element_type | solution.py:420
  90.1 0.0 copy-done.3
  90.1 2.8 %normalize.1 = (bf16[8,384,512]{2,1,0:T(8,128)(2,1)S(1)}, bf16[8,384,512]{2,1,0:T(8,128)(2,1)S(1)}) custom-call(bf16[16,384,512]{2,1,0:T(8,128)(2,1)S(1)} %bitcast.6, f32[1,8192]{1,0:T(1,128)S(1)} %copy-done.3), custom_call_target="tpu_custom_call" | custom-call | tf_op jit(solution)/shard_map/normalize/pallas_call | solution.py:181
  92.9 0.0 copy-start
  92.9 1.7 %copy-done = bf16[8,384,512]{2,1,0:T(8,128)(2,1)} copy-done((bf16[8,384,512]{2,1,0:T(8,128)(2,1)}, bf16[8,384,512]{2,1,0:T(8,128)(2,1)S(1)}, u32[]{:S(2)}) %copy-start) | copy-done | bytes 3145752
  94.6 8.4 %all-gather.5.cloned.1.call-done = bf16[8448,512]{1,0:T(8,128)(2,1)} async-done(((bf16[528,512]{1,0:T(8,128)(2,1)}), bf16[8448,512]{1,0:T(8,128)(2,1)}) %all-gather.5.cloned.1.call-update) | async-done | bytes 8650768 | tf_op jit(solution)/shard_map/all_gather | solution.py:417
  103.0 5.6 %project.1 = (bf16[384,128]{1,0:T(8,128)(2,1)S(1)}, bf16[384,256]{1,0:T(8,128)(2,1)S(1)}, bf16[384,384]{1,0:T(8,128)(2,1)S(1)}) custom-call(bf16[8,384,512]{2,1,0:T(8,128)(2,1)S(1)} %get-tuple-element.22.early_ref, bf16[8,384,512]{2,1,0:T(8,128)(2,1)} %copy-done, bf16[16,528,512]{2,1,0:T(8,128)(2,1)} %bitcast.10), custom_call_target="tpu_custom_call" | custom-call | tf_op jit(solution)/shard_map/project/pallas_call | solution.py:244
  108.6 2.6 %collective-permute-start = (bf16[384,384]{1,0:T(8,128)(2,1)S(1)}, bf16[384,384]{1,0:T(8,128)(2,1)S(1)}, u32[]{:S(2)}, u32[]{:S(2)}) collective-permute-start(bf16[384,384]{1,0:T(8,128)(2,1)S(1)} %get-tuple-element.29), channel_id=1, source_target_pairs={{0,256},{256,0},{1,257},{257,1},{2,258},{258,2},{3,259},{259,3},{4... | collective-permute-start | bytes 884744 | tf_op jit(solution)/shard_map/ppermute | solution.py:422
  111.2 0.0 copy-done.1
  111.2 0.0 copy-done.2
  111.2 1.1 plan.1.place_ref
  112.2 0.1 collective-permute-done.got_ref
  112.3 1.7 %place.1 = bf16[768,384]{1,0:T(8,128)(2,1)} custom-call(bf16[768,768]{1,0:T(8,128)(2,1)S(1)} %plan.1.place_ref, bf16[384,128]{1,0:T(8,128)(2,1)S(1)} %get-tuple-element.28.keep_ref, bf16[384,384]{1,0:T(8,128)(2,1)S(1)} %collective-permute-done.got_ref, bf16[384,256]{1,0:T(8,128)(2,1)S(1)} %get-tuple-element.30.mine_ref), custom_call_target="tpu_custom_call" | custom-call | tf_op jit(solution)/shard_map/place/pallas_call | solution.py:296
  114.0 5.0 %all-to-all-start = ((bf16[16,48,384]{2,1,0:T(8,128)(2,1)}), bf16[16,48,384]{2,1,0:T(8,128)(2,1)S(1)}, u32[]{:S(2)}, u32[]{:S(2)}) async-start(bf16[16,48,384]{2,1,0:T(8,128)(2,1)} %bitcast.2), calls=%async_computation | async-start | bytes 1179648 | tf_op jit(solution)/shard_map/all_to_all | solution.py:407
  119.0 3.7 %masks.1 = (bf16[768,768]{1,0:T(8,128)(2,1)S(1)}, bf16[768,768]{1,0:T(8,128)(2,1)S(1)}) custom-call(bf16[16,528,512]{2,1,0:T(8,128)(2,1)} %bitcast.11, s32[768]{0:T(1024)S(1)} %copy-done.1, s32[768]{0:T(1024)S(1)} %copy-done.2), custom_call_target="tpu_custom_call" | custom-call | tf_op jit(solution)/shard_map/masks/pallas_call | solution.py:349
  122.7 7.7 %all-to-all-done = bf16[16,48,384]{2,1,0:T(8,128)(2,1)S(1)} async-done(((bf16[16,48,384]{2,1,0:T(8,128)(2,1)}), bf16[16,48,384]{2,1,0:T(8,128)(2,1)S(1)}, u32[]{:S(2)}, u32[]{:S(2)}) %all-to-all-start) | async-done | bytes 589856 | tf_op jit(solution)/shard_map/all_to_all | solution.py:407
  130.4 1.8 %attend.1 = bf16[2,768,128]{2,1,0:T(8,128)(2,1)S(1)} custom-call(bf16[768,384]{1,0:T(8,128)(2,1)S(1)} %bitcast.7, bf16[768,768]{1,0:T(8,128)(2,1)S(1)} %get-tuple-element.36.bias_ref), custom_call_target="tpu_custom_call" | custom-call | tf_op jit(solution)/shard_map/attend/pallas_call | solution.py:379
  132.2 14.2 %all_to_all.10 = bf16[32,48,128]{2,1,0:T(8,128)(2,1)S(1)} all-to-all(bf16[32,48,128]{2,1,0:T(8,128)(2,1)S(1)} %bitcast.9), channel_id=1, replica_groups=mesh['tower'=2,'tp'=16,'grp'=16] {'tower','grp'}, dimensions={0} | all-to-all | bytes 786432 | tf_op jit(solution)/shard_map/all_to_all | solution.py:407
  146.4 1.2 restore.1
  (3 shorter events, 0.0 us)
Async XLA Ops:
  6.5 96.4 %all-gather.5.cloned.1.call-start = ((), (), s32[]{:S(2)}) async-start(), calls=%async_computation.2 | async-start | bytes 9191424 | tf_op jit(solution)/shard_map/all_gather | solution.py:417
  88.4 1.7 %copy-start.3 = (f32[1,8192]{1,0:T(1,128)S(1)}, f32[1,8192]{1,0:T(1,128)}, u32[]{:S(2)}) copy-start(f32[1,8192]{1,0:T(1,128)} %gain_ref.1) | copy-start | bytes 98308
  92.9 1.7 %copy-start = (bf16[8,384,512]{2,1,0:T(8,128)(2,1)}, bf16[8,384,512]{2,1,0:T(8,128)(2,1)S(1)}, u32[]{:S(2)}) copy-start(bf16[8,384,512]{2,1,0:T(8,128)(2,1)S(1)} %get-tuple-element.23.late_ref) | copy-start | bytes 9437188
  103.0 8.2 %copy-start.1 = (s32[768]{0:T(1024)S(1)}, s32[768]{0:T(1024)}, u32[]{:S(2)}) copy-start(s32[768]{0:T(1024)} %modality_ref.3) | copy-start | bytes 9220
  103.0 8.2 %copy-start.2 = (s32[768]{0:T(1024)S(1)}, s32[768]{0:T(1024)}, u32[]{:S(2)}) copy-start(s32[768]{0:T(1024)} %owner_ref.3) | copy-start | bytes 9220
  108.6 3.8 %collective-permute-start = (bf16[384,384]{1,0:T(8,128)(2,1)S(1)}, bf16[384,384]{1,0:T(8,128)(2,1)S(1)}, u32[]{:S(2)}, u32[]{:S(2)}) collective-permute-start(bf16[384,384]{1,0:T(8,128)(2,1)S(1)} %get-tuple-element.29), channel_id=1, source_target_pairs={{0,256},{256,0},{1,257},{257,1},{2,258},{258,2},{3,259},{259,3},{4... | collective-permute-start | bytes 884744 | tf_op jit(solution)/shard_map/ppermute | solution.py:422
  114.0 16.4 %all-to-all-start = ((bf16[16,48,384]{2,1,0:T(8,128)(2,1)}), bf16[16,48,384]{2,1,0:T(8,128)(2,1)S(1)}, u32[]{:S(2)}, u32[]{:S(2)}) async-start(bf16[16,48,384]{2,1,0:T(8,128)(2,1)} %bitcast.2), calls=%async_computation | async-start | bytes 1179648 | tf_op jit(solution)/shard_map/all_to_all | solution.py:407
Sparse Core Ops, SparseCore 0:
  10.4 92.5 all-gather.4

commit v5 on v4

--- a/solution.py
+++ b/solution.py
@@ -365,9 +365,9 @@
     keys, values = given_ref[:, HD : 2 * HD], given_ref[:, 2 * HD :]
     tile = min(256, tok)
     for at in range(0, tok, tile):
-        scores = dot_nt(given_ref[at : at + tile, :HD], keys) * (1.0 / math.sqrt(HD))
+        scores = dot_nt(given_ref[at : at + tile, :HD], keys) * (math.log2(math.e) / math.sqrt(HD))
         scores = scores + bias_ref[at : at + tile, :].astype(F32)
-        powered = jnp.exp(scores - jnp.max(scores, axis=1, keepdims=True))
+        powered = jnp.exp2(scores - jnp.max(scores, axis=1, keepdims=True))
         inverse = 1.0 / jnp.sum(powered, axis=1, keepdims=True)
         mixed = dot((powered * inverse).astype(BF16), values).astype(BF16)
         out_ref[0, at : at + tile, :] = mixed

time: 155 us -> 155 us (level)
  no operation moved by 1% of the time
where the time goes in v5:
time: 155 us; the launch traced here: 154 us
  blocking collectives  93.5 us (60%)
  Pallas kernels  20.2 us (13%)
  waiting for transfers between devices  16.3 us (11%)
  between operations  13.5 us (9%)
  starting transfers between devices  7.56 us (5%)
  other arithmetic  1.77 us (1%)
  local copies, waits for them, and re-layouts  1.67 us (1%)
    all_gather x1, blocking collectives, local(): gathered = lax.all_gather(lifted, 'tp', axis=0)  79.3 us
    all_to_all x1, blocking collectives, swap_all(): return lax.all_to_all(value, axes, split_axis=0, concat_axis=0, tiled=True)  14.2 us
    all_gather x1, waiting for transfers between devices, local(): weights = lax.all_gather(packed, 'grp', axis=0)  8.4 us
    all_to_all x1, waiting for transfers between devices, swap_all(): return lax.all_to_all(value, axes, split_axis=0, concat_axis=0, tiled=True)  7.74 us
    pallas_call x1, Pallas kernels, project(): pl.pallas_call(project_kernel, out_shape=(jax.ShapeDtypeStruct((half, HD)...  5.6 us
    all_to_all x1, starting transfers between devices, swap_all(): return lax.all_to_all(value, axes, split_axis=0, concat_axis=0, tiled=True)  4.98 us
    pallas_call x1, Pallas kernels, masks(): pl.pallas_call(mask_kernel, out_shape=(jax.ShapeDtypeStruct((tok, tok), B...  3.66 us
  transfers between devices with their start and end apart: 3, of which 3 were waited for; matrix products, arithmetic and copies ran while one was open for 1% of the time, Pallas kernels for 5%

profile of v5, /device:TPU:1, one launch (start us, length us, event | category | flops | bytes accessed | tf_op | source)
XLA Modules:
  0.0 154.5 jit_solution(1922306459555533126)
XLA Ops:
  6.5 0.0 all-gather.5.cloned.1.call-start
  6.5 2.4 %pack.1 = (bf16[384,512]{1,0:T(8,128)(2,1)S(1)}, bf16[528,512]{1,0:T(8,128)(2,1)}) custom-call(s32[768]{0:T(1024)} %modality_ref.3, s32[768]{0:T(1024)} %owner_ref.3, s32[768]{0:T(1024)} %doc_ref.1, bf16[768,512]{1,0:T(8,128)(2,1)} %token_ref.1, bf16[1,512,256]{2,1,0:T(8,128)(2,1)} %query_ref.1, bf16[1,512,1024]{2,1,0:T(8,128)(2,1)} %pair_ref.1), custom_call_target="tpu_custom_call" | custom-call | tf_op jit(solution)/shard_map/pack/pallas_call | solution.py:132
  9.0 0.0 all-gather.5.cloned.1.call-update
  9.0 0.1 multiply_convert_fusion.1
  9.1 79.3 %all-gather.6 = f16[6144,512]{1,0:T(8,128)(2,1)S(1)} all-gather(f16[384,512]{1,0:T(8,128)(2,1)S(1)} %multiply_convert_fusion.1), channel_id=2, replica_groups=mesh['tower'=2,'tp'=16,'grp'=16] {'tp'}, dimensions={0}, use_global_device_ids=true | all-gather | bytes 6684672 | tf_op jit(solution)/shard_map/all_gather | solution.py:419
  88.4 1.7 %multiply_convert_fusion = bf16[6144,512]{1,0:T(8,128)(2,1)S(1)} fusion(f16[6144,512]{1,0:T(8,128)(2,1)S(1)} %all-gather.6), kind=kLoop, calls=%fused_computation | loop fusion | flops 9437184 | bytes 12582912 | tf_op jit(solution)/shard_map/convert_element_type | solution.py:420
  90.1 0.0 copy-done.3
  90.1 2.8 %normalize.1 = (bf16[8,384,512]{2,1,0:T(8,128)(2,1)S(1)}, bf16[8,384,512]{2,1,0:T(8,128)(2,1)S(1)}) custom-call(bf16[16,384,512]{2,1,0:T(8,128)(2,1)S(1)} %bitcast.6, f32[1,8192]{1,0:T(1,128)S(1)} %copy-done.3), custom_call_target="tpu_custom_call" | custom-call | tf_op jit(solution)/shard_map/normalize/pallas_call | solution.py:181
  92.9 0.0 copy-start
  92.9 1.7 %copy-done = bf16[8,384,512]{2,1,0:T(8,128)(2,1)} copy-done((bf16[8,384,512]{2,1,0:T(8,128)(2,1)}, bf16[8,384,512]{2,1,0:T(8,128)(2,1)S(1)}, u32[]{:S(2)}) %copy-start) | copy-done | bytes 3145752
  94.6 8.4 %all-gather.5.cloned.1.call-done = bf16[8448,512]{1,0:T(8,128)(2,1)} async-done(((bf16[528,512]{1,0:T(8,128)(2,1)}), bf16[8448,512]{1,0:T(8,128)(2,1)}) %all-gather.5.cloned.1.call-update) | async-done | bytes 8650768 | tf_op jit(solution)/shard_map/all_gather | solution.py:417
  103.0 5.6 %project.1 = (bf16[384,128]{1,0:T(8,128)(2,1)S(1)}, bf16[384,256]{1,0:T(8,128)(2,1)S(1)}, bf16[384,384]{1,0:T(8,128)(2,1)S(1)}) custom-call(bf16[8,384,512]{2,1,0:T(8,128)(2,1)S(1)} %get-tuple-element.22.early_ref, bf16[8,384,512]{2,1,0:T(8,128)(2,1)} %copy-done, bf16[16,528,512]{2,1,0:T(8,128)(2,1)} %bitcast.10), custom_call_target="tpu_custom_call" | custom-call | tf_op jit(solution)/shard_map/project/pallas_call | solution.py:244
  108.6 2.6 %collective-permute-start = (bf16[384,384]{1,0:T(8,128)(2,1)S(1)}, bf16[384,384]{1,0:T(8,128)(2,1)S(1)}, u32[]{:S(2)}, u32[]{:S(2)}) collective-permute-start(bf16[384,384]{1,0:T(8,128)(2,1)S(1)} %get-tuple-element.29), channel_id=1, source_target_pairs={{0,256},{256,0},{1,257},{257,1},{2,258},{258,2},{3,259},{259,3},{4... | collective-permute-start | bytes 884744 | tf_op jit(solution)/shard_map/ppermute | solution.py:422
  111.2 0.0 copy-done.1
  111.2 0.0 copy-done.2
  111.2 1.1 plan.1.place_ref
  112.2 0.1 collective-permute-done.got_ref
  112.3 1.7 %place.1 = bf16[768,384]{1,0:T(8,128)(2,1)} custom-call(bf16[768,768]{1,0:T(8,128)(2,1)S(1)} %plan.1.place_ref, bf16[384,128]{1,0:T(8,128)(2,1)S(1)} %get-tuple-element.28.keep_ref, bf16[384,384]{1,0:T(8,128)(2,1)S(1)} %collective-permute-done.got_ref, bf16[384,256]{1,0:T(8,128)(2,1)S(1)} %get-tuple-element.30.mine_ref), custom_call_target="tpu_custom_call" | custom-call | tf_op jit(solution)/shard_map/place/pallas_call | solution.py:296
  114.0 5.0 %all-to-all-start = ((bf16[16,48,384]{2,1,0:T(8,128)(2,1)}), bf16[16,48,384]{2,1,0:T(8,128)(2,1)S(1)}, u32[]{:S(2)}, u32[]{:S(2)}) async-start(bf16[16,48,384]{2,1,0:T(8,128)(2,1)} %bitcast.2), calls=%async_computation | async-start | bytes 1179648 | tf_op jit(solution)/shard_map/all_to_all | solution.py:407
  119.0 3.7 %masks.1 = (bf16[768,768]{1,0:T(8,128)(2,1)S(1)}, bf16[768,768]{1,0:T(8,128)(2,1)S(1)}) custom-call(bf16[16,528,512]{2,1,0:T(8,128)(2,1)} %bitcast.11, s32[768]{0:T(1024)S(1)} %copy-done.1, s32[768]{0:T(1024)S(1)} %copy-done.2), custom_call_target="tpu_custom_call" | custom-call | tf_op jit(solution)/shard_map/masks/pallas_call | solution.py:349
  122.7 7.7 %all-to-all-done = bf16[16,48,384]{2,1,0:T(8,128)(2,1)S(1)} async-done(((bf16[16,48,384]{2,1,0:T(8,128)(2,1)}), bf16[16,48,384]{2,1,0:T(8,128)(2,1)S(1)}, u32[]{:S(2)}, u32[]{:S(2)}) %all-to-all-start) | async-done | bytes 589856 | tf_op jit(solution)/shard_map/all_to_all | solution.py:407
  130.4 1.8 %attend.1 = bf16[2,768,128]{2,1,0:T(8,128)(2,1)S(1)} custom-call(bf16[768,384]{1,0:T(8,128)(2,1)S(1)} %bitcast.7, bf16[768,768]{1,0:T(8,128)(2,1)S(1)} %get-tuple-element.36.bias_ref), custom_call_target="tpu_custom_call" | custom-call | tf_op jit(solution)/shard_map/attend/pallas_call | solution.py:379
  132.2 14.2 %all_to_all.10 = bf16[32,48,128]{2,1,0:T(8,128)(2,1)S(1)} all-to-all(bf16[32,48,128]{2,1,0:T(8,128)(2,1)S(1)} %bitcast.9), channel_id=1, replica_groups=mesh['tower'=2,'tp'=16,'grp'=16] {'tower','grp'}, dimensions={0} | all-to-all | bytes 786432 | tf_op jit(solution)/shard_map/all_to_all | solution.py:407
  146.4 1.2 restore.1
  (3 shorter events, 0.0 us)
Async XLA Ops:
  6.5 96.4 %all-gather.5.cloned.1.call-start = ((), (), s32[]{:S(2)}) async-start(), calls=%async_computation.2 | async-start | bytes 9191424 | tf_op jit(solution)/shard_map/all_gather | solution.py:417
  88.4 1.7 %copy-start.3 = (f32[1,8192]{1,0:T(1,128)S(1)}, f32[1,8192]{1,0:T(1,128)}, u32[]{:S(2)}) copy-start(f32[1,8192]{1,0:T(1,128)} %gain_ref.1) | copy-start | bytes 98308
  92.9 1.7 %copy-start = (bf16[8,384,512]{2,1,0:T(8,128)(2,1)}, bf16[8,384,512]{2,1,0:T(8,128)(2,1)S(1)}, u32[]{:S(2)}) copy-start(bf16[8,384,512]{2,1,0:T(8,128)(2,1)S(1)} %get-tuple-element.23.late_ref) | copy-start | bytes 9437188
  103.0 8.2 %copy-start.1 = (s32[768]{0:T(1024)S(1)}, s32[768]{0:T(1024)}, u32[]{:S(2)}) copy-start(s32[768]{0:T(1024)} %modality_ref.3) | copy-start | bytes 9220
  103.0 8.2 %copy-start.2 = (s32[768]{0:T(1024)S(1)}, s32[768]{0:T(1024)}, u32[]{:S(2)}) copy-start(s32[768]{0:T(1024)} %owner_ref.3) | copy-start | bytes 9220
  108.6 3.8 %collective-permute-start = (bf16[384,384]{1,0:T(8,128)(2,1)S(1)}, bf16[384,384]{1,0:T(8,128)(2,1)S(1)}, u32[]{:S(2)}, u32[]{:S(2)}) collective-permute-start(bf16[384,384]{1,0:T(8,128)(2,1)S(1)} %get-tuple-element.29), channel_id=1, source_target_pairs={{0,256},{256,0},{1,257},{257,1},{2,258},{258,2},{3,259},{259,3},{4... | collective-permute-start | bytes 884744 | tf_op jit(solution)/shard_map/ppermute | solution.py:422
  114.0 16.4 %all-to-all-start = ((bf16[16,48,384]{2,1,0:T(8,128)(2,1)}), bf16[16,48,384]{2,1,0:T(8,128)(2,1)S(1)}, u32[]{:S(2)}, u32[]{:S(2)}) async-start(bf16[16,48,384]{2,1,0:T(8,128)(2,1)} %bitcast.2), calls=%async_computation | async-start | bytes 1179648 | tf_op jit(solution)/shard_map/all_to_all | solution.py:407
Sparse Core Ops, SparseCore 0:
  10.4 92.5 all-gather.4
